TPU v7x, 32 devices: a whole 2x2x4 slice. The times are simulated.
32 devices in a mesh: groups: 2 (over y), seq: 4 (over z), head: 4 (over x, core).
Axes of the slice: x: 2, y: 2, z: 4, core: 2. Of those that a mesh axis runs over, the one named last changes fastest.
Arguments:
- query_rows: bfloat16 [4096, 2048], P(('groups', 'seq', 'head')), parts along dimension 0, may hold values from -6 to 6
- key_rows: bfloat16 [4096, 2048], P(('groups', 'seq', 'head')), parts along dimension 0, may hold values from -6 to 6
- value_rows: bfloat16 [4096, 2048], P(('groups', 'seq', 'head')), parts along dimension 0, may hold values from -24 to 24
- grad_rows: bfloat16 [4096, 2048], P(('groups', 'seq', 'head')), parts along dimension 0, may hold values from -6 to 6
- tile_offsets: int32 [8, 7, 3], P('seq'), may hold values from -1 to 1, as said below
- out_weight: bfloat16 [2048, 2048], P('seq', 'head'), may hold values from -0.125 to 0.125
Outputs:
- projected: bfloat16 [4096, 2048], P(('groups', 'seq', 'head')), parts along dimension 0
- grad_query: bfloat16 [4096, 2048], P(('groups', 'seq'), 'head'), parts along dimension 0
- grad_key: bfloat16 [4096, 2048], P(('groups', 'seq'), 'head'), parts along dimension 0
- grad_value: bfloat16 [4096, 2048], P(('groups', 'seq'), 'head'), parts along dimension 0
There are 2 independent parts, one for each index of `groups`. A program takes and returns all parts, laid end to end along the dimension named above; an argument that names none is the same for every part. Nothing has to cross between parts.
Inputs may be any that keep to these rules, and one draw needn't show every extreme that they name: tile_offsets[c, 0] is (0, 0, 0); the 7 offsets of a tile are distinct, and in each at most one of the row and column entries is nonzero.
All inputs are finite; a program needn't handle non-finite values.
Results may differ from a plain program's by a relative error of at most 0.02.
Values may be sent and summed in bfloat16 or wider, within the bound.
A program may use at most 128 MiB of HBM per device.

v0:
```python
import jax
import jax.numpy as jnp
from jax import lax
from jax.sharding import PartitionSpec as P

HEADS = 16
HEAD_DIM = 128
TILE = 256
TT = 2
TH = 2
WIN = 7


def from_behind(value, axis, steps):
    count = lax.axis_size(axis)
    first, last = (max(0, -steps), min(count, count - steps))
    return lax.ppermute(value, axis, [(source, source + steps) for source in range(first, last)])


def as_sent(shard):

    def short(part):
        return part.astype(jnp.bfloat16) if part.dtype == jnp.float32 else part

    return jax.tree.map(short, shard)


def route_of(row_step, col_step):
    return jnp.where(
        row_step == 1,
        1,
        jnp.where(row_step == -1, 2, jnp.where(col_step == 1, 3, jnp.where(col_step == -1, 4, 0))),
    ).astype(jnp.int32)


def body(query_rows, key_rows, value_rows, grad_rows, tile_offsets, out_weight):
    head_groups = lax.axis_size("head")
    seq_devices = lax.axis_size("seq")
    position = lax.axis_index("seq")
    heads_here = HEADS // head_groups
    head_width = heads_here * HEAD_DIM
    slab_rows = TT * TILE
    score_scale = HEAD_DIM ** (-0.5)
    weight_full = lax.all_gather(out_weight, "seq", axis=0, tiled=True)
    query_h, key_h, value_h, grad_h = (
        lax.all_to_all(query_rows, "head", split_axis=1, concat_axis=0, tiled=True),
        lax.all_to_all(key_rows, "head", split_axis=1, concat_axis=0, tiled=True),
        lax.all_to_all(value_rows, "head", split_axis=1, concat_axis=0, tiled=True),
        lax.all_to_all(grad_rows, "head", split_axis=1, concat_axis=0, tiled=True),
    )
    row_tile = position % TH
    col_tile = position // TH
    col_count = seq_devices // TH
    time_tile = jnp.arange(TT, dtype=jnp.int32)
    key_time = time_tile[:, None] + tile_offsets[:, :, 0]
    key_row = row_tile + tile_offsets[:, :, 1]
    key_col = col_tile + tile_offsets[:, :, 2]
    inside = (
        (key_time >= 0)
        & (key_time < TT)
        & (key_row >= 0)
        & (key_row < TH)
        & (key_col >= 0)
        & (key_col < col_count)
    )
    routes = route_of(tile_offsets[:, :, 1], tile_offsets[:, :, 2])
    target = routes * TT + jnp.clip(key_time, 0, TT - 1)
    key_value = (key_h, value_h)
    fetch_steps = (-1, 1, -TH, TH)
    blocks = [key_value] + [
        from_behind((key_value[0], key_value[1]), "seq", offset_by) for offset_by in fetch_steps
    ]
    key_buffer = jnp.stack([member[0] for member in blocks]).reshape(5 * TT, TILE, head_width)
    value_buffer = jnp.stack([member[1] for member in blocks]).reshape(5 * TT, TILE, head_width)
    query_tiles = query_h.reshape(TT, TILE, heads_here, HEAD_DIM)
    grad_tiles = grad_h.reshape(TT, TILE, heads_here, HEAD_DIM)

    def scores_of(tile_id):
        near_keys = key_buffer[target[tile_id]].reshape(WIN, TILE, heads_here, HEAD_DIM)
        near_values = value_buffer[target[tile_id]].reshape(WIN, TILE, heads_here, HEAD_DIM)
        scores = (
            jnp.einsum(
                "ihd,wjhd->hiwj",
                query_tiles[tile_id],
                near_keys,
                preferred_element_type=jnp.float32,
            )
            * score_scale
        )
        scores = jnp.where(inside[tile_id][None, None, :, None], scores, -jnp.inf)
        return (scores, near_keys, near_values)

    def forward_tile(scores, near_values):
        row_max = jnp.max(scores, axis=(2, 3), keepdims=True)
        exp_scores = jnp.exp(scores - row_max)
        row_sum = jnp.sum(exp_scores, axis=(2, 3), keepdims=True)
        weights = (exp_scores / row_sum).astype(jnp.bfloat16)
        attended = jnp.einsum(
            "hiwj,wjhd->ihd", weights, near_values, preferred_element_type=jnp.float32
        ).astype(jnp.bfloat16)
        return (weights, attended, row_max, row_sum)

    def backward_tile(tile_id, weights, attended, near_keys, near_values, sums_in):
        grad_tile = grad_tiles[tile_id]
        row_dot = jnp.sum(grad_tile.astype(jnp.float32) * attended.astype(jnp.float32), axis=-1).T
        grad_weights = jnp.einsum(
            "ihd,wjhd->hiwj", grad_tile, near_values, preferred_element_type=jnp.float32
        )
        grad_scores = (
            weights.astype(jnp.float32) * (grad_weights - row_dot[:, :, None, None])
        ).astype(jnp.bfloat16)
        query_grad = (
            score_scale
            * jnp.einsum(
                "hiwj,wjhd->ihd", grad_scores, near_keys, preferred_element_type=jnp.float32
            )
        ).astype(jnp.bfloat16)
        key_terms = score_scale * jnp.einsum(
            "hiwj,ihd->wjhd", grad_scores, query_tiles[tile_id], preferred_element_type=jnp.float32
        )
        value_terms = jnp.einsum(
            "hiwj,ihd->wjhd", weights, grad_tile, preferred_element_type=jnp.float32
        )
        key_sums, value_sums = sums_in
        key_sums = key_sums.at[target[tile_id]].add(key_terms.reshape(WIN, TILE, head_width))
        value_sums = value_sums.at[target[tile_id]].add(value_terms.reshape(WIN, TILE, head_width))
        return ((key_sums, value_sums), query_grad)

    empty_sums = jnp.zeros((5 * TT, TILE, head_width), jnp.float32)
    tile_range = jnp.arange(TT, dtype=jnp.int32)

    def joint_step(sums_in, tile_id):
        scores, near_keys, near_values = scores_of(tile_id)
        weights, attended, row_max, row_sum = forward_tile(scores, near_values)
        sums_out, query_grad = backward_tile(
            tile_id, weights, attended, near_keys, near_values, sums_in
        )
        return (sums_out, (attended, query_grad))

    (key_sums, value_sums), (attended_all, query_grads) = lax.scan(
        joint_step, (empty_sums, empty_sums), tile_range
    )
    flat_rows = attended_all.reshape(slab_rows, head_width)
    projected = lax.psum_scatter(
        lax.dot_general(
            flat_rows, weight_full, (((1,), (1,)), ((), ())), preferred_element_type=jnp.float32
        ).astype(jnp.bfloat16),
        "head",
        scatter_dimension=0,
        tiled=True,
    )
    key_parts = key_sums.reshape(5, slab_rows, head_width)
    value_parts = value_sums.reshape(5, slab_rows, head_width)
    remote = [
        (key_parts[route_id].astype(jnp.bfloat16), value_parts[route_id].astype(jnp.bfloat16))
        for route_id in range(1, 5)
    ]
    returned = [
        from_behind(as_sent(remote[route_id]), "seq", -fetch_steps[route_id])
        for route_id in range(4)
    ]
    key_total = key_parts[0]
    value_total = value_parts[0]
    for member in returned:
        key_total = key_total + member[0].astype(jnp.float32)
        value_total = value_total + member[1].astype(jnp.float32)
    grad_query = query_grads.reshape(slab_rows, head_width)
    return (projected, grad_query, key_total.astype(jnp.bfloat16), value_total.astype(jnp.bfloat16))


def solution(mesh):
    return jax.shard_map(
        body,
        mesh=mesh,
        in_specs=(
            P(("groups", "seq", "head"), None),
            P(("groups", "seq", "head"), None),
            P(("groups", "seq", "head"), None),
            P(("groups", "seq", "head"), None),
            P("seq", None, None),
            P("seq", "head"),
        ),
        out_specs=(
            P(("groups", "seq", "head"), None),
            P(("groups", "seq"), "head"),
            P(("groups", "seq"), "head"),
            P(("groups", "seq"), "head"),
        ),
        check_vma=False,
    )
```

profile of v0, /device:TPU:0, one launch (start us, length us, event | category | flops | bytes accessed | tf_op | source)
XLA Modules:
  0.0 399.0 jit_solution(17626778974556749886)
XLA Ops:
  9.6 4.3 %all-to-all-start.1 = ((bf16[128,4,512]{2,0,1:T(8,128)(2,1)}), bf16[128,4,512]{2,0,1:T(8,128)(2,1)}, u32[]{:S(2)}, u32[]{:S(2)}) async-start(bf16[128,4,512]{2,0,1:T(8,128)(2,1)} %copy.121), calls=%async_computation.1 | async-start | bytes 1048576 | tf_op jit(solution)/shard_map/all_to_all | solution.py:47
  16.2 7.1 %all-to-all-done.1 = bf16[128,4,512]{2,0,1:T(8,128)(2,1)} async-done(((bf16[128,4,512]{2,0,1:T(8,128)(2,1)}), bf16[128,4,512]{2,0,1:T(8,128)(2,1)}, u32[]{:S(2)}, u32[]{:S(2)}) %all-to-all-start.1) | async-done | bytes 524320 | tf_op jit(solution)/shard_map/all_to_all | solution.py:47
  23.4 4.1 %all-to-all-start.3 = ((bf16[128,4,512]{2,0,1:T(8,128)(2,1)}), bf16[128,4,512]{2,0,1:T(8,128)(2,1)}, u32[]{:S(2)}, u32[]{:S(2)}) async-start(bf16[128,4,512]{2,0,1:T(8,128)(2,1)} %copy.124), calls=%async_computation.3 | async-start | bytes 1048576 | tf_op jit(solution)/shard_map/all_to_all | solution.py:48
  28.4 8.1 %all-to-all-done.3 = bf16[128,4,512]{2,0,1:T(8,128)(2,1)} async-done(((bf16[128,4,512]{2,0,1:T(8,128)(2,1)}), bf16[128,4,512]{2,0,1:T(8,128)(2,1)}, u32[]{:S(2)}, u32[]{:S(2)}) %all-to-all-start.3) | async-done | bytes 524320 | tf_op jit(solution)/shard_map/all_to_all | solution.py:48
  36.4 3.5 all-to-all-start
  42.8 5.8 %collective-permute-start.1 = (bf16[512,512]{1,0:T(8,128)(2,1)}, bf16[512,512]{1,0:T(8,128)(2,1)}, u32[]{:S(2)}, u32[]{:S(2)}) collective-permute-start(bf16[512,512]{1,0:T(8,128)(2,1)} %bitcast.34), channel_id=1, source_target_pairs={{0,4},{4,8},{8,12},{1,5},{5,9},{9,13},{2,6},{6,10},{10,14},{3,7},{... | collective-permute-start | bytes 1572872 | tf_op jit(solution)/shard_map/ppermute | solution.py:17
  48.7 4.1 %all-to-all-start.2 = ((bf16[128,4,512]{2,0,1:T(8,128)(2,1)}), bf16[128,4,512]{2,0,1:T(8,128)(2,1)}, u32[]{:S(2)}, u32[]{:S(2)}) async-start(bf16[128,4,512]{2,0,1:T(8,128)(2,1)} %bitcast.174), calls=%async_computation.2 | async-start | bytes 1048576 | tf_op jit(solution)/shard_map/all_to_all | solution.py:49
  54.2 7.0 %collective-permute-start.3 = (bf16[512,512]{1,0:T(8,128)(2,1)}, bf16[512,512]{1,0:T(8,128)(2,1)}, u32[]{:S(2)}, u32[]{:S(2)}) collective-permute-start(bf16[512,512]{1,0:T(8,128)(2,1)} %bitcast.34), channel_id=1, source_target_pairs={{0,8},{4,12},{1,9},{5,13},{2,10},{6,14},{3,11},{7,15},{16,24},{20,... | collective-permute-start | bytes 1572872 | tf_op jit(solution)/shard_map/ppermute | solution.py:17
  62.5 1.9 constant_dynamic-update-slice_fusion.1
  66.7 2.0 reshape.145
  68.7 5.0 %collective-permute-start.5 = (bf16[512,512]{1,0:T(8,128)(2,1)}, bf16[512,512]{1,0:T(8,128)(2,1)S(1)}, u32[]{:S(2)}, u32[]{:S(2)}) collective-permute-start(bf16[512,512]{1,0:T(8,128)(2,1)} %bitcast.45), channel_id=1, source_target_pairs={{0,4},{4,8},{8,12},{1,5},{5,9},{9,13},{2,6},{6,10},{10,14},{3,7},{... | collective-permute-start | bytes 1572872 | tf_op jit(solution)/shard_map/ppermute | solution.py:17
  73.7 1.9 bitcast_dynamic-update-slice_fusion.7
  76.9 1.9 bitcast_dynamic-update-slice_fusion.6
  78.8 33.3 %collective-permute-done.2 = bf16[512,512]{1,0:T(8,128)(2,1)} collective-permute-done((bf16[512,512]{1,0:T(8,128)(2,1)}, bf16[512,512]{1,0:T(8,128)(2,1)}, u32[]{:S(2)}, u32[]{:S(2)}) %collective-permute-start.2) | collective-permute-done | bytes 524320 | tf_op jit(solution)/shard_map/ppermute | solution.py:17
  113.4 1.9 bitcast_dynamic-update-slice_fusion.5
  115.3 1.9 bitcast_dynamic-update-slice_fusion.4
  118.3 30.5 %collective-permute-done.6 = bf16[512,512]{1,0:T(8,128)(2,1)S(1)} collective-permute-done((bf16[512,512]{1,0:T(8,128)(2,1)}, bf16[512,512]{1,0:T(8,128)(2,1)S(1)}, u32[]{:S(2)}, u32[]{:S(2)}) %collective-permute-start.6) | collective-permute-done | bytes 524320 | tf_op jit(solution)/shard_map/ppermute | solution.py:17
  148.9 3.0 broadcast_in_dim.52
  151.9 3.0 broadcast_in_dim.52.clone
  154.9 152.1 %while.16 = (s32[]{:T(128)}, f32[10,256,512]{2,1,0:T(8,128)}, f32[10,256,512]{2,1,0:T(8,128)}, bf16[2,256,4,128]{3,2,1,0:T(4,128)(2,1)}, bf16[2,256,4,128]{3,2,1...) while((s32[]{:T(128)}, f32[10,256,512]{2,1,0:T(8,128)}, ...), condition=%wide.region_6.7_spmd, body=%wide.region_0.6_spmd.sunk | while | flops 2851600384 | bytes 200049776 | solution.py:140
  157.6 2.4 gather_fusion
  161.5 3.0 copy.200
  164.7 1.6 fusion.62
  166.3 1.5 fusion.63
  167.8 3.2 divide_convert_fusion.2
  170.9 3.7 gather_fusion.1
  174.6 4.3 %reshape.210 = bf16[7,256,4,128]{3,2,1,0:T(4,128)(2,1)} reshape(bf16[7,256,512]{2,1,0:T(8,128)(2,1)} %gather_fusion.1) | data formatting | bytes 3670016 | tf_op jit(solution)/shard_map/while/body/eval_jaxpr/reshape | solution.py:80
  178.9 4.1 %copy.201 = bf16[7,256,4,128]{1,3,0,2:T(8,128)(2,1)} copy(bf16[7,256,4,128]{3,2,1,0:T(4,128)(2,1)} %reshape.210) | data formatting | bytes 3670016 | tf_op jit(solution)/shard_map/while/body/eval_jaxpr/reshape | solution.py:80
  183.1 4.2 %multiply_reduce_fusion.2 = (f32[256,4]{0,1:T(4,128)S(1)}, bf16[4,128,256]{1,2,0:T(8,128)(2,1)S(1)}) fusion(bf16[1,256,4,128]{3,2,1,0:T(4,128)(2,1)S(1)} %constant_dynamic-slice_fusion.6, bf16[7,256,4,128]{1,3,0,2:T(8,128)(2,1)} %copy.201, bf16[4,256,7,256]{1,3,2,0:T(8,128)(2,1)} %divide_convert_fusion.2), kind=kOutput, calls=%fused_computation.18.clone.1 | convolution fusion | flops 470416384 | bytes 6033408 | tf_op jit(solution)/shard_map/while/body/eval_jaxpr/hiwj,wjhd->ihd/dot_general | solution.py:98
  188.8 1.8 copy-done.1
  192.5 3.4 multiply_bitcast_fusion.2
  195.9 2.1 copy.202
  198.0 4.6 %copy.203 = f32[7,256,512]{2,1,0:T(8,128)} copy(f32[7,256,512]{1,2,0:T(8,128)} %bitcast.228) | data formatting | bytes 7340032 | tf_op jit(solution)/shard_map/while/body/eval_jaxpr/reshape | solution.py:125
  202.6 9.1 %scatter_fusion = f32[10,256,512]{2,1,0:T(8,128)} fusion(f32[10,256,512]{2,1,0:T(8,128)} %get-tuple-element.272, s32[7]{0:T(128)S(1)} %fusion.61, f32[7,256,512]{2,1,0:T(8,128)} %copy.203), kind=kCustom, calls=%fused_computation.2.clone.1 | custom fusion | flops 917504 | bytes 11010076 | tf_op jit(solution)/shard_map/while/body/eval_jaxpr/scatter-add | solution.py:125
  211.6 3.4 convolution_bitcast_fusion.4
  215.0 2.0 copy.204
  217.0 4.6 %copy.205 = f32[7,256,512]{2,1,0:T(8,128)} copy(f32[7,256,512]{1,2,0:T(8,128)} %bitcast.229) | data formatting | bytes 7340032 | tf_op jit(solution)/shard_map/while/body/eval_jaxpr/reshape | solution.py:126
  221.6 9.3 %scatter_fusion.1 = f32[10,256,512]{2,1,0:T(8,128)} fusion(f32[10,256,512]{2,1,0:T(8,128)} %get-tuple-element.273, s32[7]{0:T(128)S(1)} %fusion.61, f32[7,256,512]{2,1,0:T(8,128)} %copy.205), kind=kCustom, calls=%fused_computation.3.clone.1 | custom fusion | flops 917504 | bytes 11010076 | tf_op jit(solution)/shard_map/while/body/eval_jaxpr/scatter-add | solution.py:126
  233.6 2.4 gather_fusion
  237.5 3.0 copy.200
  240.7 1.6 fusion.62
  243.8 3.2 divide_convert_fusion.2
  247.0 3.7 gather_fusion.1
  250.7 4.3 %reshape.210 = bf16[7,256,4,128]{3,2,1,0:T(4,128)(2,1)} reshape(bf16[7,256,512]{2,1,0:T(8,128)(2,1)} %gather_fusion.1) | data formatting | bytes 3670016 | tf_op jit(solution)/shard_map/while/body/eval_jaxpr/reshape | solution.py:80
  254.9 4.1 %copy.201 = bf16[7,256,4,128]{1,3,0,2:T(8,128)(2,1)} copy(bf16[7,256,4,128]{3,2,1,0:T(4,128)(2,1)} %reshape.210) | data formatting | bytes 3670016 | tf_op jit(solution)/shard_map/while/body/eval_jaxpr/reshape | solution.py:80
  259.1 4.2 %multiply_reduce_fusion.2 = (f32[256,4]{0,1:T(4,128)S(1)}, bf16[4,128,256]{1,2,0:T(8,128)(2,1)S(1)}) fusion(bf16[1,256,4,128]{3,2,1,0:T(4,128)(2,1)S(1)} %constant_dynamic-slice_fusion.6, bf16[7,256,4,128]{1,3,0,2:T(8,128)(2,1)} %copy.201, bf16[4,256,7,256]{1,3,2,0:T(8,128)(2,1)} %divide_convert_fusion.2), kind=kOutput, calls=%fused_computation.18.clone.1 | convolution fusion | flops 470416384 | bytes 6033408 | tf_op jit(solution)/shard_map/while/body/eval_jaxpr/hiwj,wjhd->ihd/dot_general | solution.py:98
  264.8 1.8 copy-done.1
  268.6 3.4 multiply_bitcast_fusion.2
  271.9 2.1 copy.202
  274.0 4.6 %copy.203 = f32[7,256,512]{2,1,0:T(8,128)} copy(f32[7,256,512]{1,2,0:T(8,128)} %bitcast.228) | data formatting | bytes 7340032 | tf_op jit(solution)/shard_map/while/body/eval_jaxpr/reshape | solution.py:125
  278.6 9.1 %scatter_fusion = f32[10,256,512]{2,1,0:T(8,128)} fusion(f32[10,256,512]{2,1,0:T(8,128)} %get-tuple-element.272, s32[7]{0:T(128)S(1)} %fusion.61, f32[7,256,512]{2,1,0:T(8,128)} %copy.203), kind=kCustom, calls=%fused_computation.2.clone.1 | custom fusion | flops 917504 | bytes 11010076 | tf_op jit(solution)/shard_map/while/body/eval_jaxpr/scatter-add | solution.py:125
  287.7 3.4 convolution_bitcast_fusion.4
  291.1 2.0 copy.204
  293.1 4.6 %copy.205 = f32[7,256,512]{2,1,0:T(8,128)} copy(f32[7,256,512]{1,2,0:T(8,128)} %bitcast.229) | data formatting | bytes 7340032 | tf_op jit(solution)/shard_map/while/body/eval_jaxpr/reshape | solution.py:126
  297.7 9.3 %scatter_fusion.1 = f32[10,256,512]{2,1,0:T(8,128)} fusion(f32[10,256,512]{2,1,0:T(8,128)} %get-tuple-element.273, s32[7]{0:T(128)S(1)} %fusion.61, f32[7,256,512]{2,1,0:T(8,128)} %copy.205), kind=kCustom, calls=%fused_computation.3.clone.1 | custom fusion | flops 917504 | bytes 11010076 | tf_op jit(solution)/shard_map/while/body/eval_jaxpr/scatter-add | solution.py:126
  307.0 4.4 %convolution_convert_fusion = bf16[512,2048]{1,0:T(8,128)(2,1)} fusion(bf16[2048,512]{1,0:T(8,128)(2,1)} %all-gather.2.cloned.1.call-done, bf16[64,8,4,128]{3,2,1,0:T(4,128)(2,1)} %bitcast.251), kind=kOutput, calls=%fused_computation.35 | convolution fusion | flops 1074790400 | bytes 4718592 | tf_op jit(solution)/shard_map/dot_general | solution.py:145
  311.5 3.0 convert.13
  314.6 4.6 %collective-permute-start.12 = (bf16[512,512]{1,0:T(8,128)(2,1)S(1)}, bf16[512,512]{1,0:T(8,128)(2,1)S(1)}, u32[]{:S(2)}, u32[]{:S(2)}) collective-permute-start(bf16[512,512]{1,0:T(8,128)(2,1)S(1)} %bitcast.249), channel_id=1, source_target_pairs={{0,4},{4,8},{8,12},{1,5},{5,9},{9,13},{2,6},{6,10},{10,14},{3,7},{... | collective-permute-start | bytes 1572872 | tf_op jit(solution)/shard_map/ppermute | solution.py:17
  320.6 5.1 %collective-permute-start.14 = (bf16[512,512]{1,0:T(8,128)(2,1)S(1)}, bf16[512,512]{1,0:T(8,128)(2,1)S(1)}, u32[]{:S(2)}, u32[]{:S(2)}) collective-permute-start(bf16[512,512]{1,0:T(8,128)(2,1)S(1)} %bitcast.247), channel_id=1, source_target_pairs={{0,8},{4,12},{1,9},{5,13},{2,10},{6,14},{3,11},{7,15},{16,24},{20,... | collective-permute-start | bytes 1572872 | tf_op jit(solution)/shard_map/ppermute | solution.py:17
  327.6 5.5 %collective-permute-start.10 = (bf16[512,512]{1,0:T(8,128)(2,1)S(1)}, bf16[512,512]{1,0:T(8,128)(2,1)S(1)}, u32[]{:S(2)}, u32[]{:S(2)}) collective-permute-start(bf16[512,512]{1,0:T(8,128)(2,1)S(1)} %bitcast.246), channel_id=1, source_target_pairs={{0,8},{4,12},{1,9},{5,13},{2,10},{6,14},{3,11},{7,15},{16,24},{20,... | collective-permute-start | bytes 1572872 | tf_op jit(solution)/shard_map/ppermute | solution.py:17
  334.6 26.9 %collective-permute-start.8 = (bf16[512,512]{1,0:T(8,128)(2,1)S(1)}, bf16[512,512]{1,0:T(8,128)(2,1)S(1)}, u32[]{:S(2)}, u32[]{:S(2)}) collective-permute-start(bf16[512,512]{1,0:T(8,128)(2,1)S(1)} %bitcast.244), channel_id=1, source_target_pairs={{0,4},{4,8},{8,12},{1,5},{5,9},{9,13},{2,6},{6,10},{10,14},{3,7},{... | collective-permute-start | bytes 1572872 | tf_op jit(solution)/shard_map/ppermute | solution.py:17
  365.1 5.3 %collective-permute-done.15 = bf16[512,512]{1,0:T(8,128)(2,1)S(1)} collective-permute-done((bf16[512,512]{1,0:T(8,128)(2,1)S(1)}, bf16[512,512]{1,0:T(8,128)(2,1)S(1)}, u32[]{:S(2)}, u32[]{:S(2)}) %collective-permute-start.15) | collective-permute-done | bytes 524320 | tf_op jit(solution)/shard_map/ppermute | solution.py:17
  371.5 10.0 %collective-permute-done.11 = bf16[512,512]{1,0:T(8,128)(2,1)S(1)} collective-permute-done((bf16[512,512]{1,0:T(8,128)(2,1)S(1)}, bf16[512,512]{1,0:T(8,128)(2,1)S(1)}, u32[]{:S(2)}, u32[]{:S(2)}) %collective-permute-start.11) | collective-permute-done | bytes 524320 | tf_op jit(solution)/shard_map/ppermute | solution.py:17
  381.5 9.5 %collective-permute-done.9 = bf16[512,512]{1,0:T(8,128)(2,1)S(1)} collective-permute-done((bf16[512,512]{1,0:T(8,128)(2,1)S(1)}, bf16[512,512]{1,0:T(8,128)(2,1)S(1)}, u32[]{:S(2)}, u32[]{:S(2)}) %collective-permute-start.9) | collective-permute-done | bytes 524320 | tf_op jit(solution)/shard_map/ppermute | solution.py:17
  (113 shorter events, 41.0 us)
Async XLA Ops:
  7.2 20.3 %copy-start.7 = (bf16[128,2048]{1,0:T(8,128)(2,1)S(1)}, bf16[128,2048]{1,0:T(8,128)(2,1)}, u32[]{:S(2)}) copy-start(bf16[128,2048]{1,0:T(8,128)(2,1)} %param.8) | copy-start | bytes 1572868
  9.6 32.4 %copy-start.10 = (s32[2,7,3]{1,0,2:T(2,128)S(1)}, s32[2,7,3]{1,0,2:T(2,128)}, u32[]{:S(2)}) copy-start(s32[2,7,3]{1,0,2:T(2,128)} %param.12) | copy-start | bytes 508
  9.6 32.4 %copy-start.8 = (bf16[128,2048]{1,0:T(8,128)(2,1)S(1)}, bf16[128,2048]{1,0:T(8,128)(2,1)}, u32[]{:S(2)}) copy-start(bf16[128,2048]{1,0:T(8,128)(2,1)} %param.11) | copy-start | bytes 1572868
  9.6 13.8 %all-to-all-start.1 = ((bf16[128,4,512]{2,0,1:T(8,128)(2,1)}), bf16[128,4,512]{2,0,1:T(8,128)(2,1)}, u32[]{:S(2)}, u32[]{:S(2)}) async-start(bf16[128,4,512]{2,0,1:T(8,128)(2,1)} %copy.121), calls=%async_computation.1 | async-start | bytes 1048576 | tf_op jit(solution)/shard_map/all_to_all | solution.py:47
  23.4 13.1 %all-to-all-start.3 = ((bf16[128,4,512]{2,0,1:T(8,128)(2,1)}), bf16[128,4,512]{2,0,1:T(8,128)(2,1)}, u32[]{:S(2)}, u32[]{:S(2)}) async-start(bf16[128,4,512]{2,0,1:T(8,128)(2,1)} %copy.124), calls=%async_computation.3 | async-start | bytes 1048576 | tf_op jit(solution)/shard_map/all_to_all | solution.py:48
  36.4 12.3 %all-to-all-start = ((bf16[128,4,512]{2,0,1:T(8,128)(2,1)}), bf16[128,4,512]{2,0,1:T(8,128)(2,1)S(1)}, u32[]{:S(2)}, u32[]{:S(2)}) async-start(bf16[128,4,512]{2,0,1:T(8,128)(2,1)} %bitcast.175), calls=%async_computation | async-start | bytes 1048576 | tf_op jit(solution)/shard_map/all_to_all | solution.py:46
  39.9 267.1 %all-gather.2.cloned.1.call-start = ((), (), s32[]{:S(2)}) async-start(), calls=%async_computation.5 | async-start | bytes 2621440 | tf_op jit(solution)/shard_map/all_gather | solution.py:44
  40.6 28.0 %collective-permute-start = (bf16[512,512]{1,0:T(8,128)(2,1)}, bf16[512,512]{1,0:T(8,128)(2,1)}, u32[]{:S(2)}, u32[]{:S(2)}) collective-permute-start(bf16[512,512]{1,0:T(8,128)(2,1)} %bitcast.34), channel_id=1, source_target_pairs={{4,0},{8,4},{12,8},{5,1},{9,5},{13,9},{6,2},{10,6},{14,10},{7,3},{... | collective-permute-start | bytes 1572872 | tf_op jit(solution)/shard_map/ppermute | solution.py:17
  42.8 32.8 %collective-permute-start.1 = (bf16[512,512]{1,0:T(8,128)(2,1)}, bf16[512,512]{1,0:T(8,128)(2,1)}, u32[]{:S(2)}, u32[]{:S(2)}) collective-permute-start(bf16[512,512]{1,0:T(8,128)(2,1)} %bitcast.34), channel_id=1, source_target_pairs={{0,4},{4,8},{8,12},{1,5},{5,9},{9,13},{2,6},{6,10},{10,14},{3,7},{... | collective-permute-start | bytes 1572872 | tf_op jit(solution)/shard_map/ppermute | solution.py:17
  48.7 16.8 %copy-start.6 = (bf16[128,4,512]{2,0,1:T(8,128)(2,1)}, bf16[128,4,512]{2,0,1:T(8,128)(2,1)S(1)}, u32[]{:S(2)}) copy-start(bf16[128,4,512]{2,0,1:T(8,128)(2,1)S(1)} %all-to-all-done) | copy-start | bytes 1572868
  48.7 18.0 %all-to-all-start.2 = ((bf16[128,4,512]{2,0,1:T(8,128)(2,1)}), bf16[128,4,512]{2,0,1:T(8,128)(2,1)}, u32[]{:S(2)}, u32[]{:S(2)}) async-start(bf16[128,4,512]{2,0,1:T(8,128)(2,1)} %bitcast.174), calls=%async_computation.2 | async-start | bytes 1048576 | tf_op jit(solution)/shard_map/all_to_all | solution.py:49
  52.9 339.3 %reduce-scatter.2.cloned.1.call-start = ((), (), s32[]{:S(2)}) async-start(), calls=%async_computation.6 | async-start | bytes 2621440 | tf_op jit(solution)/shard_map/reduce_scatter | solution.py:144
  52.9 59.1 %collective-permute-start.2 = (bf16[512,512]{1,0:T(8,128)(2,1)}, bf16[512,512]{1,0:T(8,128)(2,1)}, u32[]{:S(2)}, u32[]{:S(2)}) collective-permute-start(bf16[512,512]{1,0:T(8,128)(2,1)} %bitcast.34), channel_id=1, source_target_pairs={{8,0},{12,4},{9,1},{13,5},{10,2},{14,6},{11,3},{15,7},{24,16},{28,... | collective-permute-start | bytes 1572872 | tf_op jit(solution)/shard_map/ppermute | solution.py:17
  54.2 61.0 %collective-permute-start.3 = (bf16[512,512]{1,0:T(8,128)(2,1)}, bf16[512,512]{1,0:T(8,128)(2,1)}, u32[]{:S(2)}, u32[]{:S(2)}) collective-permute-start(bf16[512,512]{1,0:T(8,128)(2,1)} %bitcast.34), channel_id=1, source_target_pairs={{0,8},{4,12},{1,9},{5,13},{2,10},{6,14},{3,11},{7,15},{16,24},{20,... | collective-permute-start | bytes 1572872 | tf_op jit(solution)/shard_map/ppermute | solution.py:17
  61.3 55.9 %collective-permute-start.4 = (bf16[512,512]{1,0:T(8,128)(2,1)}, bf16[512,512]{1,0:T(8,128)(2,1)}, u32[]{:S(2)}, u32[]{:S(2)}) collective-permute-start(bf16[512,512]{1,0:T(8,128)(2,1)} %bitcast.45), channel_id=1, source_target_pairs={{4,0},{8,4},{12,8},{5,1},{9,5},{13,9},{6,2},{10,6},{14,10},{7,3},{... | collective-permute-start | bytes 1572872 | tf_op jit(solution)/shard_map/ppermute | solution.py:17
  68.7 49.6 %collective-permute-start.5 = (bf16[512,512]{1,0:T(8,128)(2,1)}, bf16[512,512]{1,0:T(8,128)(2,1)S(1)}, u32[]{:S(2)}, u32[]{:S(2)}) collective-permute-start(bf16[512,512]{1,0:T(8,128)(2,1)} %bitcast.45), channel_id=1, source_target_pairs={{0,4},{4,8},{8,12},{1,5},{5,9},{9,13},{2,6},{6,10},{10,14},{3,7},{... | collective-permute-start | bytes 1572872 | tf_op jit(solution)/shard_map/ppermute | solution.py:17
  75.6 73.2 %collective-permute-start.6 = (bf16[512,512]{1,0:T(8,128)(2,1)}, bf16[512,512]{1,0:T(8,128)(2,1)S(1)}, u32[]{:S(2)}, u32[]{:S(2)}) collective-permute-start(bf16[512,512]{1,0:T(8,128)(2,1)} %bitcast.45), channel_id=1, source_target_pairs={{8,0},{12,4},{9,1},{13,5},{10,2},{14,6},{11,3},{15,7},{24,16},{28,... | collective-permute-start | bytes 1572872 | tf_op jit(solution)/shard_map/ppermute | solution.py:17
  112.1 36.7 %collective-permute-start.7 = (bf16[512,512]{1,0:T(8,128)(2,1)}, bf16[512,512]{1,0:T(8,128)(2,1)S(1)}, u32[]{:S(2)}, u32[]{:S(2)}) collective-permute-start(bf16[512,512]{1,0:T(8,128)(2,1)} %bitcast.45), channel_id=1, source_target_pairs={{0,8},{4,12},{1,9},{5,13},{2,10},{6,14},{3,11},{7,15},{16,24},{20,... | collective-permute-start | bytes 1572872 | tf_op jit(solution)/shard_map/ppermute | solution.py:17
  154.9 2.7 copy-start.3
  174.6 8.4 %copy-start.5 = (bf16[2,256,4,128]{3,2,1,0:T(4,128)(2,1)S(1)}, bf16[2,256,4,128]{3,2,1,0:T(4,128)(2,1)}, u32[]{:S(2)}) copy-start(bf16[2,256,4,128]{3,2,1,0:T(4,128)(2,1)} %get-tuple-element.296) | copy-start | bytes 1572868 | tf_op jit(solution)/shard_map/while
  183.1 4.2 %copy-start = (bf16[4,256,7,256]{1,3,2,0:T(8,128)(2,1)S(1)}, bf16[4,256,7,256]{1,3,2,0:T(8,128)(2,1)}, u32[]{:S(2)}) copy-start(bf16[4,256,7,256]{1,3,2,0:T(8,128)(2,1)} %divide_convert_fusion.2) | copy-start | bytes 11010052 | tf_op jit(solution)/shard_map/while
  183.1 4.2 %copy-start.2 = (bf16[7,256,4,128]{1,3,0,2:T(8,128)(2,1)S(1)}, bf16[7,256,4,128]{1,3,0,2:T(8,128)(2,1)}, u32[]{:S(2)}) copy-start(bf16[7,256,4,128]{1,3,0,2:T(8,128)(2,1)} %copy.201) | copy-start | bytes 5505028 | tf_op jit(solution)/shard_map/while
  188.7 1.8 copy-start.1
  221.6 9.3 %copy-start.4 = (bf16[10,256,512]{2,1,0:T(8,128)(2,1)S(1)}, bf16[10,256,512]{2,1,0:T(8,128)(2,1)}, u32[]{:S(2)}) copy-start(bf16[10,256,512]{2,1,0:T(8,128)(2,1)} %copy-done.3) | copy-start | bytes 7864324 | tf_op jit(solution)/shard_map/while
  230.9 2.7 copy-start.3
  250.7 8.4 %copy-start.5 = (bf16[2,256,4,128]{3,2,1,0:T(4,128)(2,1)S(1)}, bf16[2,256,4,128]{3,2,1,0:T(4,128)(2,1)}, u32[]{:S(2)}) copy-start(bf16[2,256,4,128]{3,2,1,0:T(4,128)(2,1)} %get-tuple-element.296) | copy-start | bytes 1572868 | tf_op jit(solution)/shard_map/while
  259.1 4.2 %copy-start = (bf16[4,256,7,256]{1,3,2,0:T(8,128)(2,1)S(1)}, bf16[4,256,7,256]{1,3,2,0:T(8,128)(2,1)}, u32[]{:S(2)}) copy-start(bf16[4,256,7,256]{1,3,2,0:T(8,128)(2,1)} %divide_convert_fusion.2) | copy-start | bytes 11010052 | tf_op jit(solution)/shard_map/while
  259.1 4.2 %copy-start.2 = (bf16[7,256,4,128]{1,3,0,2:T(8,128)(2,1)S(1)}, bf16[7,256,4,128]{1,3,0,2:T(8,128)(2,1)}, u32[]{:S(2)}) copy-start(bf16[7,256,4,128]{1,3,0,2:T(8,128)(2,1)} %copy.201) | copy-start | bytes 5505028 | tf_op jit(solution)/shard_map/while
  264.8 1.8 copy-start.1
  297.7 9.3 %copy-start.4 = (bf16[10,256,512]{2,1,0:T(8,128)(2,1)S(1)}, bf16[10,256,512]{2,1,0:T(8,128)(2,1)}, u32[]{:S(2)}) copy-start(bf16[10,256,512]{2,1,0:T(8,128)(2,1)} %copy-done.3) | copy-start | bytes 7864324 | tf_op jit(solution)/shard_map/while
  311.4 15.5 %slice-start = ((s8[5242880]{0:T(1024)(128)(4,1)}), s8[1048576]{0:T(1024)(128)(4,1)S(1)}, s32[]{:S(2)}) async-start(s8[5242880]{0:T(1024)(128)(4,1)} %bitcast.230), calls=%async_computation.7 | async-start | bytes 2097152
  311.5 15.5 %slice-start.1 = ((s8[5242880]{0:T(1024)(128)(4,1)}), s8[4194304]{0:T(1024)(128)(4,1)S(1)}, s32[]{:S(2)}) async-start(s8[5242880]{0:T(1024)(128)(4,1)} %bitcast.230), calls=%async_computation.8 | async-start | bytes 8388608
  314.6 18.5 %collective-permute-start.12 = (bf16[512,512]{1,0:T(8,128)(2,1)S(1)}, bf16[512,512]{1,0:T(8,128)(2,1)S(1)}, u32[]{:S(2)}, u32[]{:S(2)}) collective-permute-start(bf16[512,512]{1,0:T(8,128)(2,1)S(1)} %bitcast.249), channel_id=1, source_target_pairs={{0,4},{4,8},{8,12},{1,5},{5,9},{9,13},{2,6},{6,10},{10,14},{3,7},{... | collective-permute-start | bytes 1572872 | tf_op jit(solution)/shard_map/ppermute | solution.py:17
  319.2 15.4 %collective-permute-start.13 = (bf16[512,512]{1,0:T(8,128)(2,1)S(1)}, bf16[512,512]{1,0:T(8,128)(2,1)S(1)}, u32[]{:S(2)}, u32[]{:S(2)}) collective-permute-start(bf16[512,512]{1,0:T(8,128)(2,1)S(1)} %bitcast.248), channel_id=1, source_target_pairs={{4,0},{8,4},{12,8},{5,1},{9,5},{13,9},{6,2},{10,6},{14,10},{7,3},{... | collective-permute-start | bytes 1572872 | tf_op jit(solution)/shard_map/ppermute | solution.py:17
  320.6 41.0 %collective-permute-start.14 = (bf16[512,512]{1,0:T(8,128)(2,1)S(1)}, bf16[512,512]{1,0:T(8,128)(2,1)S(1)}, u32[]{:S(2)}, u32[]{:S(2)}) collective-permute-start(bf16[512,512]{1,0:T(8,128)(2,1)S(1)} %bitcast.247), channel_id=1, source_target_pairs={{0,8},{4,12},{1,9},{5,13},{2,10},{6,14},{3,11},{7,15},{16,24},{20,... | collective-permute-start | bytes 1572872 | tf_op jit(solution)/shard_map/ppermute | solution.py:17
  325.7 44.7 %collective-permute-start.15 = (bf16[512,512]{1,0:T(8,128)(2,1)S(1)}, bf16[512,512]{1,0:T(8,128)(2,1)S(1)}, u32[]{:S(2)}, u32[]{:S(2)}) collective-permute-start(bf16[512,512]{1,0:T(8,128)(2,1)S(1)} %bitcast.242), channel_id=1, source_target_pairs={{8,0},{12,4},{9,1},{13,5},{10,2},{14,6},{11,3},{15,7},{24,16},{28,... | collective-permute-start | bytes 1572872 | tf_op jit(solution)/shard_map/ppermute | solution.py:17
  327.4 36.8 %copy-start.9 = (bf16[2,256,4,128]{3,2,1,0:T(4,128)(2,1)S(1)}, bf16[2,256,4,128]{3,2,1,0:T(4,128)(2,1)}, u32[]{:S(2)}) copy-start(bf16[2,256,4,128]{3,2,1,0:T(4,128)(2,1)} %get-tuple-element.70) | copy-start | bytes 1572868
  327.6 43.9 %collective-permute-start.10 = (bf16[512,512]{1,0:T(8,128)(2,1)S(1)}, bf16[512,512]{1,0:T(8,128)(2,1)S(1)}, u32[]{:S(2)}, u32[]{:S(2)}) collective-permute-start(bf16[512,512]{1,0:T(8,128)(2,1)S(1)} %bitcast.246), channel_id=1, source_target_pairs={{0,8},{4,12},{1,9},{5,13},{2,10},{6,14},{3,11},{7,15},{16,24},{20,... | collective-permute-start | bytes 1572872 | tf_op jit(solution)/shard_map/ppermute | solution.py:17
  333.1 48.4 %collective-permute-start.11 = (bf16[512,512]{1,0:T(8,128)(2,1)S(1)}, bf16[512,512]{1,0:T(8,128)(2,1)S(1)}, u32[]{:S(2)}, u32[]{:S(2)}) collective-permute-start(bf16[512,512]{1,0:T(8,128)(2,1)S(1)} %bitcast.245), channel_id=1, source_target_pairs={{8,0},{12,4},{9,1},{13,5},{10,2},{14,6},{11,3},{15,7},{24,16},{28,... | collective-permute-start | bytes 1572872 | tf_op jit(solution)/shard_map/ppermute | solution.py:17
  334.6 46.9 %collective-permute-start.8 = (bf16[512,512]{1,0:T(8,128)(2,1)S(1)}, bf16[512,512]{1,0:T(8,128)(2,1)S(1)}, u32[]{:S(2)}, u32[]{:S(2)}) collective-permute-start(bf16[512,512]{1,0:T(8,128)(2,1)S(1)} %bitcast.244), channel_id=1, source_target_pairs={{0,4},{4,8},{8,12},{1,5},{5,9},{9,13},{2,6},{6,10},{10,14},{3,7},{... | collective-permute-start | bytes 1572872 | tf_op jit(solution)/shard_map/ppermute | solution.py:17
  361.5 29.5 %collective-permute-start.9 = (bf16[512,512]{1,0:T(8,128)(2,1)S(1)}, bf16[512,512]{1,0:T(8,128)(2,1)S(1)}, u32[]{:S(2)}, u32[]{:S(2)}) collective-permute-start(bf16[512,512]{1,0:T(8,128)(2,1)S(1)} %bitcast.243), channel_id=1, source_target_pairs={{4,0},{8,4},{12,8},{5,1},{9,5},{13,9},{6,2},{10,6},{14,10},{7,3},{... | collective-permute-start | bytes 1572872 | tf_op jit(solution)/shard_map/ppermute | solution.py:17
Sparse Core Ops, SparseCore 0:
  42.3 87.6 all-gather.1
  311.6 33.9 reduce-scatter.1
where the time goes:
time: 401 us; the launch traced here: 399 us
  waiting for transfers between devices  105 us (26%)
  local copies, waits for them, and re-layouts  102 us (25%)
  starting transfers between devices  87.7 us (22%)
  other arithmetic  51.9 us (13%)
  matrix products  33.6 us (8%)
  between operations  14.5 us (4%)
  loops' own time  4.24 us (1%)
    ppermute x16, waiting for transfers between devices, from_behind(): lax.ppermute(value, axis, [(source, source + steps) for source in range(f...  88.7 us
    ppermute x16, starting transfers between devices, from_behind(): lax.ppermute(value, axis, [(source, source + steps) for source in range(f...  71.5 us
    scatter-add x2, other arithmetic, backward_tile(): value_sums.at[target[tile_id]]  18.6 us
    scatter-add x2, other arithmetic, backward_tile(): key_sums.at[target[tile_id]].add(key_terms.reshape(WIN, TILE, head_width))  18.2 us
    reshape x4, local copies, waits for them, and re-layouts, scores_of(): value_buffer[target[tile_id]].reshape(WIN, TILE, heads_here, HEAD_DIM)  16.7 us
    unnamed x25, local copies, waits for them, and re-layouts  13.4 us
    reshape x2, local copies, waits for them, and re-layouts, backward_tile(): key_terms.reshape(WIN, TILE, head_width)  9.18 us
    reshape x2, local copies, waits for them, and re-layouts, backward_tile(): value_terms.reshape(WIN, TILE, head_width)  9.13 us
  transfers between devices with their start and end apart: 22, of which 9 were waited for; matrix products, arithmetic and copies ran while one was open for 44% of the time, Pallas kernels for 0%

commit v1 on v0

v1 whole, which is shorter than its diff:
```python
import functools

import jax
import jax.numpy as jnp
from jax import lax
from jax.experimental import pallas as pl
from jax.experimental.pallas import tpu as pltpu
from jax.sharding import PartitionSpec as P

HEADS = 16
HEAD_DIM = 128
TILE = 256
TT = 2
TH = 2
SCALE = HEAD_DIM ** (-0.5)
DEAD = -1e30


def dot(a, b, ca, cb):
    return lax.dot_general(a, b, (((ca,), (cb,)), ((), ())), preferred_element_type=jnp.float32)


def live_bias(tile_offsets, position, steps):
    row_tile, col_tile = position % TH, position // TH
    query_time = jnp.arange(TT, dtype=jnp.int32)
    rows = []
    for step_r, step_c, there in steps(row_tile, col_tile):
        for key_time in range(TT):
            hit = (
                (tile_offsets[:, :, 0] == key_time - query_time[:, None])
                & (tile_offsets[:, :, 1] == step_r)
                & (tile_offsets[:, :, 2] == step_c)
            )
            rows.append(jnp.any(hit, axis=1) & there)
    live = jnp.stack(rows)
    return jnp.repeat(jnp.where(live, 0.0, DEAD).astype(jnp.float32), TILE, axis=1)


def one_head(q, g, key_of, value_of, bias_ref, blocks, s_scr, w_scr, put_key, put_value):
    top = None
    for b in range(blocks):
        s = dot(key_of(b), q, 1, 1) * SCALE + bias_ref[b : b + 1, :]
        s_scr[b] = s
        high = jnp.max(s, axis=0, keepdims=True)
        top = high if top is None else jnp.maximum(top, high)
    total = None
    for b in range(blocks):
        p = jnp.exp(s_scr[b] - top)
        s_scr[b] = p
        part = jnp.sum(p, axis=0, keepdims=True)
        total = part if total is None else total + part
    share = 1.0 / total
    att = None
    for b in range(blocks):
        w = (s_scr[b] * share).astype(jnp.bfloat16)
        w_scr[b] = w
        part = dot(value_of(b), w, 0, 0)
        att = part if att is None else att + part
        put_value(b, dot(w, g, 1, 0))
    att = att.astype(jnp.bfloat16).astype(jnp.float32)
    row_dot = jnp.sum(att * g.astype(jnp.float32).T, axis=0, keepdims=True)
    dq = None
    for b in range(blocks):
        dw = dot(value_of(b), g, 1, 1)
        ds = (w_scr[b].astype(jnp.float32) * (dw - row_dot)).astype(jnp.bfloat16)
        part = dot(key_of(b), ds, 0, 0)
        dq = part if dq is None else dq + part
        put_key(b, dot(ds, q, 1, 0) * SCALE)
    return att.T.astype(jnp.bfloat16), (dq * SCALE).T.astype(jnp.bfloat16)


def attend_kernel(routes, *refs):
    bias_ref, q_ref, g_ref = refs[:3]
    k_refs, v_refs = refs[3 : 3 + routes], refs[3 + routes : 3 + 2 * routes]
    outs = refs[3 + 2 * routes :]
    att_ref, dq_ref = outs[:2]
    dk_refs, dv_refs = outs[2 : 2 + routes], outs[2 + routes : 2 + 2 * routes]
    s_scr, w_scr = outs[2 + 2 * routes :]

    def rows(b):
        return slice((b % TT) * TILE, (b % TT + 1) * TILE)

    def put(refs_of):
        def store(b, value):
            refs_of[b // TT][rows(b), :] = value.astype(refs_of[b // TT].dtype)

        return store

    att_ref[...], dq_ref[...] = one_head(
        q_ref[...],
        g_ref[...],
        lambda b: k_refs[b // TT][rows(b), :],
        lambda b: v_refs[b // TT][rows(b), :],
        bias_ref,
        routes * TT,
        s_scr,
        w_scr,
        put(dk_refs),
        put(dv_refs),
    )


def attend(bias, query, grad, keys, values):
    routes = len(keys)
    slab, width = query.shape
    block = pl.BlockSpec((slab, HEAD_DIM), lambda h: (0, h))
    sums = [jax.ShapeDtypeStruct((slab, width), jnp.float32 if r == 0 else jnp.bfloat16) for r in range(routes)]
    like = jax.ShapeDtypeStruct((slab, width), jnp.bfloat16)
    outs = pl.pallas_call(
        functools.partial(attend_kernel, routes),
        grid=(width // HEAD_DIM,),
        in_specs=[pl.BlockSpec(bias.shape, lambda h: (0, 0))] + [block] * (2 + 2 * routes),
        out_specs=[block] * (2 + 2 * routes),
        out_shape=[like, like] + sums + sums,
        scratch_shapes=[
            pltpu.VMEM((routes * TT, TILE, slab), jnp.float32),
            pltpu.VMEM((routes * TT, TILE, slab), jnp.bfloat16),
        ],
        compiler_params=pltpu.CompilerParams(vmem_limit_bytes=48 * 2**20),
        name="attend",
    )(bias, query, grad, *keys, *values)
    return outs[0], outs[1], outs[2 : 2 + routes], outs[2 + routes :]


def routes_of(col_count):
    seq = col_count * TH
    moves = [[(s, s ^ 1) for s in range(seq)]]
    if col_count == 2:
        moves.append([(s, s ^ TH) for s in range(seq)])
    else:
        moves.append([(s, s + TH) for s in range(seq - TH)])
        moves.append([(s, s - TH) for s in range(TH, seq)])

    def steps(row_tile, col_tile):
        found = [(0, 0, True), (1 - 2 * row_tile, 0, True)]
        if col_count == 2:
            found.append((0, 1 - 2 * col_tile, True))
        else:
            found += [(0, -1, col_tile > 0), (0, 1, col_tile < col_count - 1)]
        return found

    return moves, steps


def body(query_rows, key_rows, value_rows, grad_rows, tile_offsets, out_weight):
    seq = lax.axis_size("seq")
    moves, steps = routes_of(seq // TH)
    bias = live_bias(tile_offsets, lax.axis_index("seq"), steps)
    weight = lax.all_gather(out_weight, "seq", axis=0, tiled=True)
    key_h, value_h, query_h, grad_h = (
        lax.all_to_all(rows, "head", split_axis=1, concat_axis=0, tiled=True)
        for rows in (key_rows, value_rows, query_rows, grad_rows)
    )
    keys = [key_h] + [lax.ppermute(key_h, "seq", move) for move in moves]
    values = [value_h] + [lax.ppermute(value_h, "seq", move) for move in moves]
    att, dq, dk, dv = attend(bias, query_h, grad_h, keys, values)
    projected = lax.psum_scatter(
        dot(att, weight, 1, 1).astype(jnp.bfloat16), "head", scatter_dimension=0, tiled=True
    )

    def settle(terms):
        total = terms[0]
        for term, move in zip(terms[1:], moves):
            back = [(t, s) for s, t in move]
            total = total + lax.ppermute(term, "seq", back).astype(jnp.float32)
        return total.astype(jnp.bfloat16)

    return projected, dq, settle(dk), settle(dv)


def solution(mesh):
    return jax.shard_map(
        body,
        mesh=mesh,
        in_specs=(
            P(("groups", "seq", "head"), None),
            P(("groups", "seq", "head"), None),
            P(("groups", "seq", "head"), None),
            P(("groups", "seq", "head"), None),
            P("seq", None, None),
            P("seq", "head"),
        ),
        out_specs=(
            P(("groups", "seq", "head"), None),
            P(("groups", "seq"), "head"),
            P(("groups", "seq"), "head"),
            P(("groups", "seq"), "head"),
        ),
        check_vma=False,
    )
```

time: 401 us -> 187 us (0.47)
  local copies, waits for them, and re-layouts: 102 us -> 9.57 us
  starting transfers between devices: 87.7 us -> 25.7 us
  other arithmetic: 51.9 us -> 3.51 us
  matrix products: 33.6 us -> 4.36 us
  Pallas kernels: 0 us -> 17.3 us
  waiting for transfers between devices: 105 us -> 112 us
  loops' own time: 4.24 us -> 0 us
    ppermute x16 -> x8, starting transfers between devices: 71.5 us -> 10.8 us  [the longest x4 5.52 us: settle(): total = total + lax.ppermute(term, 'seq', back).astype(jnp.float32)]
    reshape x14 -> x0, local copies, waits for them, and re-layouts: 47.2 us -> none  [the longest x4 16.7 us: scores_of(): value_buffer[target[tile_id]].reshape(WIN, TILE, heads_here, HEAD_DIM)]
    scatter-add x4 -> x0, other arithmetic: 36.8 us -> none  [the longest x2 18.6 us: backward_tile(): value_sums.at[target[tile_id]]]
    dot_general x13 -> x1, matrix products: 33.6 us -> 4.36 us  [dot(): lax.dot_general(a, b, (((ca,), (cb,)), ((), ())), preferred_element_type=...]
    pallas_call x0 -> x1, Pallas kernels: none -> 17.3 us  [attend(): pl.pallas_call(functools.partial(attend_kernel, routes), grid=(width // H...]
    gather x4 -> x0, local copies, waits for them, and re-layouts: 12.2 us -> none  [the longest x2 7.35 us: scores_of(): value_buffer[target[tile_id]].reshape(WIN, TILE, heads_here, HEAD_DIM)]
    all_to_all x4, waiting for transfers between devices: 15.3 us -> 26.9 us  [body(): lax.all_to_all(rows, 'head', split_axis=1, concat_axis=0, tiled=True)]
    unnamed x25 -> x30, local copies, waits for them, and re-layouts: 13.4 us -> 5.08 us
  transfers between devices with their start and end apart: 22 -> 14, of which waited for: 9 -> 10; matrix products, arithmetic and copies ran while one was open for 44% -> 4% of each run, Pallas kernels for 0% -> 9%
where the time goes in v1:
time: 187 us
  waiting for transfers between devices  112 us (60%)
  starting transfers between devices  25.7 us (14%)
  Pallas kernels  17.3 us (9%)
  between operations  14.2 us (8%)
  local copies, waits for them, and re-layouts  9.57 us (5%)
  matrix products  4.36 us (2%)
  other arithmetic  3.51 us (2%)
    ppermute x4, waiting for transfers between devices, settle(): total = total + lax.ppermute(term, 'seq', back).astype(jnp.float32)  42.9 us
    all_to_all x4, waiting for transfers between devices, body(): lax.all_to_all(rows, 'head', split_axis=1, concat_axis=0, tiled=True)  26.9 us
    ppermute x2, waiting for transfers between devices, body(): values = [value_h] + [lax.ppermute(value_h, 'seq', move) for move in moves]  22.1 us
    ppermute x2, waiting for transfers between devices, body(): keys = [key_h] + [lax.ppermute(key_h, 'seq', move) for move in moves]  19.5 us
    pallas_call x1, Pallas kernels, attend(): pl.pallas_call(functools.partial(attend_kernel, routes), grid=(width // H...  17.3 us
    all_to_all x4, starting transfers between devices, body(): lax.all_to_all(rows, 'head', split_axis=1, concat_axis=0, tiled=True)  14.8 us
    ppermute x4, starting transfers between devices, settle(): total = total + lax.ppermute(term, 'seq', back).astype(jnp.float32)  5.52 us
    unnamed x30, local copies, waits for them, and re-layouts  5.08 us
  transfers between devices with their start and end apart: 14, of which 10 were waited for; matrix products, arithmetic and copies ran while one was open for 4% of the time, Pallas kernels for 9%

profile of v1, /device:TPU:0, one launch (start us, length us, event | category | flops | bytes accessed | tf_op | source)
XLA Modules:
  0.0 186.6 jit_solution(12280765001941788465)
XLA Ops:
  7.2 0.0 copy-start.10
  7.2 0.0 all-gather.2.cloned.1.call-start
  7.2 0.7 all-gather.2.cloned.1.call-update
  7.9 0.0 copy-start.11
  7.9 1.9 %copy.24 = bf16[16,4,8,512]{3,2,0,1:T(8,128)(2,1)} copy(bf16[16,4,8,512]{3,2,1,0:T(8,128)(2,1)} %bitcast.90) | data formatting | bytes 1048576 | tf_op jit(solution)/shard_map/all_to_all | solution.py:151
  9.9 0.0 copy-start.13
  9.9 4.3 %all-to-all-start.2 = ((bf16[128,4,512]{2,0,1:T(8,128)(2,1)}), bf16[128,4,512]{2,0,1:T(8,128)(2,1)S(1)}, u32[]{:S(2)}, u32[]{:S(2)}) async-start(bf16[128,4,512]{2,0,1:T(8,128)(2,1)} %bitcast.77), calls=%async_computation.2 | async-start | bytes 1048576 | tf_op jit(solution)/shard_map/all_to_all | solution.py:151
  14.2 0.0 copy-done.10
  14.2 0.0 copy-start.12
  14.2 0.8 copy.23
  15.0 8.0 %all-to-all-done.2 = bf16[128,4,512]{2,0,1:T(8,128)(2,1)S(1)} async-done(((bf16[128,4,512]{2,0,1:T(8,128)(2,1)}), bf16[128,4,512]{2,0,1:T(8,128)(2,1)S(1)}, u32[]{:S(2)}, u32[]{:S(2)}) %all-to-all-start.2) | async-done | bytes 524320 | tf_op jit(solution)/shard_map/all_to_all | solution.py:151
  23.0 3.5 %all-to-all-start.3 = ((bf16[128,4,512]{2,0,1:T(8,128)(2,1)}), bf16[128,4,512]{2,0,1:T(8,128)(2,1)S(1)}, u32[]{:S(2)}, u32[]{:S(2)}) async-start(bf16[128,4,512]{2,0,1:T(8,128)(2,1)} %bitcast.76), calls=%async_computation.3 | async-start | bytes 1048576 | tf_op jit(solution)/shard_map/all_to_all | solution.py:151
  26.5 0.0 copy-done.11
  26.5 0.8 copy.26
  27.4 0.0 copy-done.13
  27.4 8.0 %all-to-all-done.3 = bf16[128,4,512]{2,0,1:T(8,128)(2,1)S(1)} async-done(((bf16[128,4,512]{2,0,1:T(8,128)(2,1)}), bf16[128,4,512]{2,0,1:T(8,128)(2,1)S(1)}, u32[]{:S(2)}, u32[]{:S(2)}) %all-to-all-start.3) | async-done | bytes 524320 | tf_op jit(solution)/shard_map/all_to_all | solution.py:151
  35.3 3.5 %all-to-all-start = ((bf16[128,4,512]{2,0,1:T(8,128)(2,1)}), bf16[128,4,512]{2,0,1:T(8,128)(2,1)S(1)}, u32[]{:S(2)}, u32[]{:S(2)}) async-start(bf16[128,4,512]{2,0,1:T(8,128)(2,1)} %bitcast.79), calls=%async_computation | async-start | bytes 1048576 | tf_op jit(solution)/shard_map/all_to_all | solution.py:151
  38.9 0.0 copy-done.12
  38.9 0.8 copy.25
  39.7 0.1 bitcast_compare_fusion.1
  39.8 2.3 %collective-permute-start = (bf16[512,512]{1,0:T(8,128)(2,1)S(1)}, bf16[512,512]{1,0:T(8,128)(2,1)S(1)}, u32[]{:S(2)}, u32[]{:S(2)}) collective-permute-start(bf16[512,512]{1,0:T(8,128)(2,1)S(1)} %bitcast.80), channel_id=1, source_target_pairs={{0,4},{4,0},{8,12},{12,8},{1,5},{5,1},{9,13},{13,9},{2,6},{6,2},{1... | collective-permute-start | bytes 1572872 | tf_op jit(solution)/shard_map/ppermute | solution.py:154
  42.0 2.6 %collective-permute-start.1 = (bf16[512,512]{1,0:T(8,128)(2,1)S(1)}, bf16[512,512]{1,0:T(8,128)(2,1)S(1)}, u32[]{:S(2)}, u32[]{:S(2)}) collective-permute-start(bf16[512,512]{1,0:T(8,128)(2,1)S(1)} %bitcast.81), channel_id=1, source_target_pairs={{0,8},{4,12},{8,0},{12,4},{1,9},{5,13},{9,1},{13,5},{2,10},{6,14},... | collective-permute-start | bytes 1572872 | tf_op jit(solution)/shard_map/ppermute | solution.py:154
  44.6 0.5 collective-permute-start.2
  45.1 0.0 collective-permute-start.3
  45.1 0.2 fusion.1
  45.3 2.3 %all-to-all-done = bf16[128,4,512]{2,0,1:T(8,128)(2,1)S(1)} async-done(((bf16[128,4,512]{2,0,1:T(8,128)(2,1)}), bf16[128,4,512]{2,0,1:T(8,128)(2,1)S(1)}, u32[]{:S(2)}, u32[]{:S(2)}) %all-to-all-start) | async-done | bytes 524320 | tf_op jit(solution)/shard_map/all_to_all | solution.py:151
  47.6 3.5 %all-to-all-start.1 = ((bf16[128,4,512]{2,0,1:T(8,128)(2,1)}), bf16[128,4,512]{2,0,1:T(8,128)(2,1)S(1)}, u32[]{:S(2)}, u32[]{:S(2)}) async-start(bf16[128,4,512]{2,0,1:T(8,128)(2,1)} %bitcast.89), calls=%async_computation.1 | async-start | bytes 1048576 | tf_op jit(solution)/shard_map/all_to_all | solution.py:151
  51.1 0.0 reduce-scatter.2.cloned.1.call-start
  51.2 0.1 broadcast_bitcast_fusion
  51.3 8.7 %all-to-all-done.1 = bf16[128,4,512]{2,0,1:T(8,128)(2,1)S(1)} async-done(((bf16[128,4,512]{2,0,1:T(8,128)(2,1)}), bf16[128,4,512]{2,0,1:T(8,128)(2,1)S(1)}, u32[]{:S(2)}, u32[]{:S(2)}) %all-to-all-start.1) | async-done | bytes 524320 | tf_op jit(solution)/shard_map/all_to_all | solution.py:151
  59.9 19.5 %collective-permute-done.refs_4_ = bf16[512,512]{1,0:T(8,128)(2,1)S(1)} collective-permute-done((bf16[512,512]{1,0:T(8,128)(2,1)S(1)}, bf16[512,512]{1,0:T(8,128)(2,1)S(1)}, u32[]{:S(2)}, u32[]{:S(2)}) %collective-permute-start) | collective-permute-done | bytes 524320 | tf_op jit(solution)/shard_map/ppermute | solution.py:154
  79.4 0.0 collective-permute-done.1.refs_5_
  79.4 22.1 %collective-permute-done.2.refs_7_ = bf16[512,512]{1,0:T(8,128)(2,1)} collective-permute-done((bf16[512,512]{1,0:T(8,128)(2,1)S(1)}, bf16[512,512]{1,0:T(8,128)(2,1)}, u32[]{:S(2)}, u32[]{:S(2)}) %collective-permute-start.2) | collective-permute-done | bytes 524320 | tf_op jit(solution)/shard_map/ppermute | solution.py:155
  101.5 0.0 collective-permute-done.3.refs_8_
  101.5 17.3 %attend.1 = (bf16[512,512]{1,0:T(8,128)(2,1)S(1)}, bf16[512,512]{1,0:T(8,128)(2,1)}, f32[512,512]{1,0:T(8,128)}, bf16[512,512]{1,0:T(8,128)(2,1)S(1)}, bf16[512,...) custom-call(f32[6,512]{1,0:T(8,128)S(1)} %bitcast.88, ...), custom_call_target="tpu_custom_call" | custom-call | tf_op jit(solution)/shard_map/attend/pallas_call | solution.py:109
  118.8 0.0 copy-start
  118.8 0.8 copy-done
  119.6 0.0 copy-start.2
  119.6 0.8 copy-done.2
  120.3 0.0 copy-start.4
  120.4 0.8 copy-done.4
  121.1 0.0 copy-start.6
  121.1 0.8 copy-done.6
  121.9 0.0 copy-start.8
  122.0 0.8 copy-done.8
  122.7 0.0 all-gather.2.cloned.1.call-done
  122.7 4.4 %convolution_convert_fusion = bf16[512,2048]{1,0:T(8,128)(2,1)} fusion(bf16[512,512]{1,0:T(8,128)(2,1)} %copy-done.8, bf16[2048,512]{1,0:T(8,128)(2,1)} %all-gather.2.cloned.1.call-done), kind=kOutput, calls=%fused_computation | convolution fusion | flops 1074790400 | bytes 4718592 | tf_op jit(solution)/shard_map/dot_general | solution.py:20
  127.1 0.0 copy-start.9
  127.1 0.0 reduce-scatter.2.cloned.1.call-update
  127.2 1.0 copy-done.7
  128.1 2.4 %collective-permute-start.6 = (bf16[512,512]{1,0:T(8,128)(2,1)S(1)}, bf16[512,512]{1,0:T(8,128)(2,1)S(1)}, u32[]{:S(2)}, u32[]{:S(2)}) collective-permute-start(bf16[512,512]{1,0:T(8,128)(2,1)S(1)} %copy-done.7), channel_id=1, source_target_pairs={{4,0},{0,4},{12,8},{8,12},{5,1},{1,5},{13,9},{9,13},{6,2},{2,6},{1... | collective-permute-start | bytes 1572872 | tf_op jit(solution)/shard_map/ppermute | solution.py:165
  130.6 0.0 copy-done.5
  130.6 0.5 collective-permute-start.7
  131.1 0.0 copy-done.3
  131.1 0.7 collective-permute-start.4
  131.8 0.0 copy-done.1
  131.8 1.9 %collective-permute-start.5 = (bf16[512,512]{1,0:T(8,128)(2,1)S(1)}, bf16[512,512]{1,0:T(8,128)(2,1)S(1)}, u32[]{:S(2)}, u32[]{:S(2)}) collective-permute-start(bf16[512,512]{1,0:T(8,128)(2,1)S(1)} %copy-done.1), channel_id=1, source_target_pairs={{8,0},{12,4},{0,8},{4,12},{9,1},{13,5},{1,9},{5,13},{10,2},{14,6},... | collective-permute-start | bytes 1572872 | tf_op jit(solution)/shard_map/ppermute | solution.py:165
  133.7 18.8 %collective-permute-done.6 = bf16[512,512]{1,0:T(8,128)(2,1)S(1)} collective-permute-done((bf16[512,512]{1,0:T(8,128)(2,1)S(1)}, bf16[512,512]{1,0:T(8,128)(2,1)S(1)}, u32[]{:S(2)}, u32[]{:S(2)}) %collective-permute-start.6) | collective-permute-done | bytes 524320 | tf_op jit(solution)/shard_map/ppermute | solution.py:165
  152.5 5.2 %collective-permute-done.7 = bf16[512,512]{1,0:T(8,128)(2,1)S(1)} collective-permute-done((bf16[512,512]{1,0:T(8,128)(2,1)S(1)}, bf16[512,512]{1,0:T(8,128)(2,1)S(1)}, u32[]{:S(2)}, u32[]{:S(2)}) %collective-permute-start.7) | collective-permute-done | bytes 524320 | tf_op jit(solution)/shard_map/ppermute | solution.py:165
  157.7 2.2 %add_convert_fusion = bf16[512,512]{1,0:T(8,128)(2,1)} fusion(bf16[512,512]{1,0:T(8,128)(2,1)S(1)} %collective-permute-done.7, f32[512,512]{1,0:T(8,128)} %get-tuple-element.17, bf16[512,512]{1,0:T(8,128)(2,1)S(1)} %collective-permute-done.6), kind=kLoop, calls=%fused_computation.1 | loop fusion | flops 1310720 | bytes 2621440 | tf_op jit(solution)/shard_map/convert_element_type | solution.py:166
  159.9 14.4 %collective-permute-done.4 = bf16[512,512]{1,0:T(8,128)(2,1)S(1)} collective-permute-done((bf16[512,512]{1,0:T(8,128)(2,1)S(1)}, bf16[512,512]{1,0:T(8,128)(2,1)S(1)}, u32[]{:S(2)}, u32[]{:S(2)}) %collective-permute-start.4) | collective-permute-done | bytes 524320 | tf_op jit(solution)/shard_map/ppermute | solution.py:165
  174.3 4.5 %collective-permute-done.5 = bf16[512,512]{1,0:T(8,128)(2,1)S(1)} collective-permute-done((bf16[512,512]{1,0:T(8,128)(2,1)S(1)}, bf16[512,512]{1,0:T(8,128)(2,1)S(1)}, u32[]{:S(2)}, u32[]{:S(2)}) %collective-permute-start.5) | collective-permute-done | bytes 524320 | tf_op jit(solution)/shard_map/ppermute | solution.py:165
  178.8 0.0 copy-done.9
  178.8 1.0 add_convert_fusion.1
  (10 shorter events, 0.1 us)
Async XLA Ops:
  7.2 7.0 %copy-start.10 = (bf16[128,2048]{1,0:T(8,128)(2,1)S(1)}, bf16[128,2048]{1,0:T(8,128)(2,1)}, u32[]{:S(2)}) copy-start(bf16[128,2048]{1,0:T(8,128)(2,1)} %param.8) | copy-start | bytes 1572868
  7.2 115.6 %all-gather.2.cloned.1.call-start = ((), (), s32[]{:S(2)}) async-start(), calls=%async_computation.5 | async-start | bytes 2621440 | tf_op jit(solution)/shard_map/all_gather | solution.py:149
  7.9 18.6 %copy-start.11 = (bf16[128,2048]{1,0:T(8,128)(2,1)S(1)}, bf16[128,2048]{1,0:T(8,128)(2,1)}, u32[]{:S(2)}) copy-start(bf16[128,2048]{1,0:T(8,128)(2,1)} %param.6) | copy-start | bytes 1572868
  9.9 17.5 %copy-start.13 = (s32[2,7,3]{1,0,2:T(2,128)S(1)}, s32[2,7,3]{1,0,2:T(2,128)}, u32[]{:S(2)}) copy-start(s32[2,7,3]{1,0,2:T(2,128)} %param.10) | copy-start | bytes 508
  9.9 13.2 %all-to-all-start.2 = ((bf16[128,4,512]{2,0,1:T(8,128)(2,1)}), bf16[128,4,512]{2,0,1:T(8,128)(2,1)S(1)}, u32[]{:S(2)}, u32[]{:S(2)}) async-start(bf16[128,4,512]{2,0,1:T(8,128)(2,1)} %bitcast.77), calls=%async_computation.2 | async-start | bytes 1048576 | tf_op jit(solution)/shard_map/all_to_all | solution.py:151
  14.2 24.7 %copy-start.12 = (bf16[128,2048]{1,0:T(8,128)(2,1)S(1)}, bf16[128,2048]{1,0:T(8,128)(2,1)}, u32[]{:S(2)}) copy-start(bf16[128,2048]{1,0:T(8,128)(2,1)} %param.9) | copy-start | bytes 1572868
  23.0 12.3 %all-to-all-start.3 = ((bf16[128,4,512]{2,0,1:T(8,128)(2,1)}), bf16[128,4,512]{2,0,1:T(8,128)(2,1)S(1)}, u32[]{:S(2)}, u32[]{:S(2)}) async-start(bf16[128,4,512]{2,0,1:T(8,128)(2,1)} %bitcast.76), calls=%async_computation.3 | async-start | bytes 1048576 | tf_op jit(solution)/shard_map/all_to_all | solution.py:151
  35.3 12.3 %all-to-all-start = ((bf16[128,4,512]{2,0,1:T(8,128)(2,1)}), bf16[128,4,512]{2,0,1:T(8,128)(2,1)S(1)}, u32[]{:S(2)}, u32[]{:S(2)}) async-start(bf16[128,4,512]{2,0,1:T(8,128)(2,1)} %bitcast.79), calls=%async_computation | async-start | bytes 1048576 | tf_op jit(solution)/shard_map/all_to_all | solution.py:151
  39.8 39.6 %collective-permute-start = (bf16[512,512]{1,0:T(8,128)(2,1)S(1)}, bf16[512,512]{1,0:T(8,128)(2,1)S(1)}, u32[]{:S(2)}, u32[]{:S(2)}) collective-permute-start(bf16[512,512]{1,0:T(8,128)(2,1)S(1)} %bitcast.80), channel_id=1, source_target_pairs={{0,4},{4,0},{8,12},{12,8},{1,5},{5,1},{9,13},{13,9},{2,6},{6,2},{1... | collective-permute-start | bytes 1572872 | tf_op jit(solution)/shard_map/ppermute | solution.py:154
  42.0 37.4 %collective-permute-start.1 = (bf16[512,512]{1,0:T(8,128)(2,1)S(1)}, bf16[512,512]{1,0:T(8,128)(2,1)S(1)}, u32[]{:S(2)}, u32[]{:S(2)}) collective-permute-start(bf16[512,512]{1,0:T(8,128)(2,1)S(1)} %bitcast.81), channel_id=1, source_target_pairs={{0,8},{4,12},{8,0},{12,4},{1,9},{5,13},{9,1},{13,5},{2,10},{6,14},... | collective-permute-start | bytes 1572872 | tf_op jit(solution)/shard_map/ppermute | solution.py:154
  44.6 56.8 %collective-permute-start.2 = (bf16[512,512]{1,0:T(8,128)(2,1)S(1)}, bf16[512,512]{1,0:T(8,128)(2,1)}, u32[]{:S(2)}, u32[]{:S(2)}) collective-permute-start(bf16[512,512]{1,0:T(8,128)(2,1)S(1)} %bitcast.83), channel_id=1, source_target_pairs={{0,4},{4,0},{8,12},{12,8},{1,5},{5,1},{9,13},{13,9},{2,6},{6,2},{1... | collective-permute-start | bytes 1572872 | tf_op jit(solution)/shard_map/ppermute | solution.py:155
  45.1 56.4 %collective-permute-start.3 = (bf16[512,512]{1,0:T(8,128)(2,1)S(1)}, bf16[512,512]{1,0:T(8,128)(2,1)}, u32[]{:S(2)}, u32[]{:S(2)}) collective-permute-start(bf16[512,512]{1,0:T(8,128)(2,1)S(1)} %bitcast.84), channel_id=1, source_target_pairs={{0,8},{4,12},{8,0},{12,4},{1,9},{5,13},{9,1},{13,5},{2,10},{6,14},... | collective-permute-start | bytes 1572872 | tf_op jit(solution)/shard_map/ppermute | solution.py:155
  47.6 12.3 %all-to-all-start.1 = ((bf16[128,4,512]{2,0,1:T(8,128)(2,1)}), bf16[128,4,512]{2,0,1:T(8,128)(2,1)S(1)}, u32[]{:S(2)}, u32[]{:S(2)}) async-start(bf16[128,4,512]{2,0,1:T(8,128)(2,1)} %bitcast.89), calls=%async_computation.1 | async-start | bytes 1048576 | tf_op jit(solution)/shard_map/all_to_all | solution.py:151
  51.1 128.7 %reduce-scatter.2.cloned.1.call-start = ((), (), s32[]{:S(2)}) async-start(), calls=%async_computation.6 | async-start | bytes 2621440 | tf_op jit(solution)/shard_map/reduce_scatter | solution.py:157
  118.8 0.8 copy-start
  119.6 0.8 copy-start.2
  120.3 0.8 copy-start.4
  121.1 0.8 copy-start.6
  121.9 0.8 copy-start.8
  127.1 1.0 copy-start.7
  127.1 3.5 %copy-start.5 = (bf16[512,512]{1,0:T(8,128)(2,1)S(1)}, bf16[512,512]{1,0:T(8,128)(2,1)}, u32[]{:S(2)}) copy-start(bf16[512,512]{1,0:T(8,128)(2,1)} %copy-done.4) | copy-start | bytes 1572868
  127.1 4.0 %copy-start.3 = (bf16[512,512]{1,0:T(8,128)(2,1)S(1)}, bf16[512,512]{1,0:T(8,128)(2,1)}, u32[]{:S(2)}) copy-start(bf16[512,512]{1,0:T(8,128)(2,1)} %copy-done.2) | copy-start | bytes 1572868
  127.1 4.7 %copy-start.1 = (bf16[512,512]{1,0:T(8,128)(2,1)S(1)}, bf16[512,512]{1,0:T(8,128)(2,1)}, u32[]{:S(2)}) copy-start(bf16[512,512]{1,0:T(8,128)(2,1)} %copy-done) | copy-start | bytes 1572868
  127.1 51.7 %copy-start.9 = (f32[512,512]{1,0:T(8,128)S(1)}, f32[512,512]{1,0:T(8,128)}, u32[]{:S(2)}) copy-start(f32[512,512]{1,0:T(8,128)} %get-tuple-element.14) | copy-start | bytes 3145732
  128.1 24.4 %collective-permute-start.6 = (bf16[512,512]{1,0:T(8,128)(2,1)S(1)}, bf16[512,512]{1,0:T(8,128)(2,1)S(1)}, u32[]{:S(2)}, u32[]{:S(2)}) collective-permute-start(bf16[512,512]{1,0:T(8,128)(2,1)S(1)} %copy-done.7), channel_id=1, source_target_pairs={{4,0},{0,4},{12,8},{8,12},{5,1},{1,5},{13,9},{9,13},{6,2},{2,6},{1... | collective-permute-start | bytes 1572872 | tf_op jit(solution)/shard_map/ppermute | solution.py:165
  130.6 27.1 %collective-permute-start.7 = (bf16[512,512]{1,0:T(8,128)(2,1)S(1)}, bf16[512,512]{1,0:T(8,128)(2,1)S(1)}, u32[]{:S(2)}, u32[]{:S(2)}) collective-permute-start(bf16[512,512]{1,0:T(8,128)(2,1)S(1)} %copy-done.5), channel_id=1, source_target_pairs={{8,0},{12,4},{0,8},{4,12},{9,1},{13,5},{1,9},{5,13},{10,2},{14,6},... | collective-permute-start | bytes 1572872 | tf_op jit(solution)/shard_map/ppermute | solution.py:165
  131.1 43.2 %collective-permute-start.4 = (bf16[512,512]{1,0:T(8,128)(2,1)S(1)}, bf16[512,512]{1,0:T(8,128)(2,1)S(1)}, u32[]{:S(2)}, u32[]{:S(2)}) collective-permute-start(bf16[512,512]{1,0:T(8,128)(2,1)S(1)} %copy-done.3), channel_id=1, source_target_pairs={{4,0},{0,4},{12,8},{8,12},{5,1},{1,5},{13,9},{9,13},{6,2},{2,6},{1... | collective-permute-start | bytes 1572872 | tf_op jit(solution)/shard_map/ppermute | solution.py:165
  131.8 47.0 %collective-permute-start.5 = (bf16[512,512]{1,0:T(8,128)(2,1)S(1)}, bf16[512,512]{1,0:T(8,128)(2,1)S(1)}, u32[]{:S(2)}, u32[]{:S(2)}) collective-permute-start(bf16[512,512]{1,0:T(8,128)(2,1)S(1)} %copy-done.1), channel_id=1, source_target_pairs={{8,0},{12,4},{0,8},{4,12},{9,1},{13,5},{1,9},{5,13},{10,2},{14,6},... | collective-permute-start | bytes 1572872 | tf_op jit(solution)/shard_map/ppermute | solution.py:165
Sparse Core Ops, SparseCore 0:
  9.6 64.7 all-gather.1
  127.3 31.5 reduce-scatter.1

commit v2 on v1

--- a/solution.py
+++ b/solution.py
@@ -142,10 +142,281 @@
     return moves, steps
 
 
+MESH = pl.DeviceIdType.MESH
+
+
+def whole_kernel(groups, seq, head, *refs):
+    bias_ref, k_in, v_in, q_in, g_in, w_in = refs[:6]
+    proj_ref, dq_ref, dk_ref, dv_ref = refs[6:10]
+    mine, near, d_self, d_out, d_in, att, weight, p_out, p_in, p_self, s_scr, w_scr = refs[10:22]
+    (x_send, x_recv, x_own, n_send, n_recv, d_send, d_recv, z_send, z_recv, y_send, y_recv, w_own, p_send, p_recv) = refs[22:]
+    inputs = (k_in, v_in, q_in, g_in)
+    heads, slab = mine.shape[1], mine.shape[2]
+    rows = k_in.shape[0]
+    half = weight.shape[2]
+    width = heads * HEAD_DIM
+    me_g, me_s, me_h = lax.axis_index("groups"), lax.axis_index("seq"), lax.axis_index("head")
+    beside = (me_s + 1 - 2 * lax.rem(me_s, TH), lax.rem(me_s + TH, seq))
+
+    def at(g=None, s=None, h=None):
+        return (me_g if g is None else g, me_s if s is None else s, me_h if h is None else h)
+
+    def after(i):
+        return lax.rem(me_h + i, head)
+
+    def before(i):
+        return lax.rem(me_h + head - i, head)
+
+    def remote(src, dst, send, recv, device):
+        return pltpu.make_async_remote_copy(
+            src_ref=src, dst_ref=dst, send_sem=send, recv_sem=recv, device_id=device, device_id_type=MESH
+        )
+
+    def columns(owner, h):
+        return pl.ds(pl.multiple_of(owner * width + h * HEAD_DIM, HEAD_DIM), HEAD_DIM)
+
+    def row_block(owner):
+        return pl.ds(pl.multiple_of(owner * rows, rows), rows)
+
+    def head_move(a, h, i, owner):
+        return remote(
+            inputs[a].at[:, columns(after(i), h)],
+            mine.at[a, h, row_block(owner), :],
+            x_send.at[a, h, i - 1],
+            x_recv.at[a, h, i - 1],
+            at(h=after(i)),
+        )
+
+    def head_own(a, h):
+        return pltpu.make_async_copy(
+            inputs[a].at[:, columns(me_h, h)], mine.at[a, h, row_block(me_h), :], x_own.at[a, h]
+        )
+
+    def near_move(j, a, h):
+        return remote(mine.at[a, h], near.at[j, a, h], n_send.at[j, a, h], n_recv.at[j, a, h], at(s=beside[j]))
+
+    def grad_move(j, a, h):
+        return remote(d_out.at[j, a, h], d_in.at[j, a, h], d_send.at[j, a, h], d_recv.at[j, a, h], at(s=beside[j]))
+
+    def weight_z(i, owner):
+        return remote(
+            w_in.at[pl.ds(pl.multiple_of(me_g * half, half), half), :],
+            weight.at[owner, me_g],
+            z_send.at[i - 1],
+            z_recv.at[i - 1],
+            at(s=lax.rem(me_s + i, seq)),
+        )
+
+    def weight_y(i, part):
+        owner = lax.rem(me_s + seq - i, seq)
+        return remote(
+            weight.at[owner, me_g], weight.at[owner, part], y_send.at[i - 1], y_recv.at[i - 1], at(g=1 - me_g)
+        )
+
+    def weight_own(part):
+        return pltpu.make_async_copy(
+            w_in.at[pl.ds(part * half, half), :], weight.at[me_s, part], w_own.at[part]
+        )
+
+    def term_move(i):
+        return remote(p_out.at[i - 1], p_in.at[i - 1], p_send.at[i - 1], p_recv.at[i - 1], at(h=after(i)))
+
+    barrier = pltpu.get_barrier_semaphore()
+    peers = [at(h=after(i)) for i in range(1, head)]
+    peers += [at(s=lax.rem(me_s + i, seq)) for i in range(1, seq)] + [at(g=1 - me_g)]
+    for peer in peers:
+        pl.semaphore_signal(barrier, inc=1, device_id=peer, device_id_type=MESH)
+    pl.semaphore_wait(barrier, len(peers))
+
+    def send_inputs(pair):
+        def step(h, carry):
+            for i in range(1, head):
+                for a in pair:
+                    head_move(a, h, i, me_h).start()
+            for a in pair:
+                head_own(a, h).start()
+            return carry
+
+        lax.fori_loop(0, heads, step, 0)
+
+    def take_inputs(a, h):
+        for i in range(1, head):
+            head_move(a, h, i, before(i)).wait_recv()
+        head_own(a, h).wait()
+
+    send_inputs((0, 1))
+    for i in range(1, seq):
+        weight_z(i, me_s).start()
+    send_inputs((2, 3))
+    for part in range(2):
+        weight_own(part).start()
+
+    def pass_on(h, carry):
+        for a in range(2):
+            take_inputs(a, h)
+            for j in (1, 0):
+                near_move(j, a, h).start()
+        return carry
+
+    lax.fori_loop(0, heads, pass_on, 0)
+    for i in range(1, seq):
+        weight_z(i, lax.rem(me_s + seq - i, seq)).wait_recv()
+        weight_y(i, me_g).start()
+
+    def work(h, carry):
+        take_inputs(2, h)
+        take_inputs(3, h)
+        for j in range(2):
+            for a in range(2):
+                near_move(j, a, h).wait_recv()
+
+        def tile(b):
+            return slice((b % TT) * TILE, (b % TT + 1) * TILE)
+
+        def read(a):
+            def of(b):
+                r = b // TT
+                return mine[a, h, tile(b), :] if r == 0 else near[r - 1, a, h, tile(b), :]
+
+            return of
+
+        def put(a):
+            def store(b, value):
+                r = b // TT
+                if r == 0:
+                    d_self[a, h, tile(b), :] = value
+                else:
+                    d_out[r - 1, a, h, tile(b), :] = value.astype(jnp.bfloat16)
+
+            return store
+
+        attended, dq = one_head(
+            mine[2, h], mine[3, h], read(0), read(1), bias_ref, 3 * TT, s_scr, w_scr, put(0), put(1)
+        )
+        att[:, columns(0, h)] = attended
+        dq_ref[:, columns(0, h)] = dq
+        for a in range(2):
+            for j in (1, 0):
+                grad_move(j, a, h).start()
+        return carry
+
+    lax.fori_loop(0, heads, work, 0)
+
+    for part in range(2):
+        weight_own(part).wait()
+    for i in range(1, seq):
+        weight_y(i, 1 - me_g).wait_recv()
+
+    def project(owner, store):
+        lines = att[row_block(owner), :]
+        for s in range(seq):
+            for part in range(2):
+                start = (s * 2 + part) * half
+                store(slice(start, start + half), dot(lines, weight[s, part], 1, 1))
+
+    for i in range(1, head):
+
+        def to_send(cols, value, i=i):
+            p_out[i - 1, :, cols] = value.astype(jnp.bfloat16)
+
+        project(after(i), to_send)
+        term_move(i).start()
+
+    def to_keep(cols, value):
+        p_self[:, cols] = value
+
+    project(me_h, to_keep)
+
+    def settle(h, carry):
+        for a, out in ((1, dv_ref), (0, dk_ref)):
+            total = d_self[a, h]
+            for j in range(2):
+                grad_move(j, a, h).wait_recv()
+                total = total + d_in[j, a, h].astype(jnp.float32)
+            out[:, columns(0, h)] = total.astype(jnp.bfloat16)
+        return carry
+
+    lax.fori_loop(0, heads, settle, 0)
+    for i in range(1, head):
+        term_move(i).wait_recv()
+    total = p_self[...]
+    for i in range(1, head):
+        total = total + p_in[i - 1].astype(jnp.float32)
+    proj_ref[...] = total.astype(jnp.bfloat16)
+
+    def drain(h, carry):
+        for a in range(4):
+            for i in range(1, head):
+                head_move(a, h, i, me_h).wait_send()
+        for a in range(2):
+            for j in range(2):
+                near_move(j, a, h).wait_send()
+                grad_move(j, a, h).wait_send()
+        return carry
+
+    lax.fori_loop(0, heads, drain, 0)
+    for i in range(1, seq):
+        weight_z(i, me_s).wait_send()
+        weight_y(i, me_g).wait_send()
+    for i in range(1, head):
+        term_move(i).wait_send()
+
+
+def whole(bias, key_rows, value_rows, query_rows, grad_rows, out_weight):
+    groups, seq, head = (lax.axis_size(name) for name in ("groups", "seq", "head"))
+    rows, features = key_rows.shape
+    slab, width = rows * head, features // head
+    heads = width // HEAD_DIM
+    half = out_weight.shape[0] // 2
+    b16, f32, dma = jnp.bfloat16, jnp.float32, pltpu.SemaphoreType.DMA
+    vmem = pl.BlockSpec(memory_space=pltpu.VMEM)
+    grads = jax.ShapeDtypeStruct((slab, width), b16)
+    return pl.pallas_call(
+        functools.partial(whole_kernel, groups, seq, head),
+        in_specs=[vmem] + [pl.BlockSpec(memory_space=pl.ANY)] * 5,
+        out_specs=[vmem] * 4,
+        out_shape=[jax.ShapeDtypeStruct((rows, features), b16), grads, grads, grads],
+        scratch_shapes=[
+            pltpu.VMEM((4, heads, slab, HEAD_DIM), b16),
+            pltpu.VMEM((2, 2, heads, slab, HEAD_DIM), b16),
+            pltpu.VMEM((2, heads, slab, HEAD_DIM), f32),
+            pltpu.VMEM((2, 2, heads, slab, HEAD_DIM), b16),
+            pltpu.VMEM((2, 2, heads, slab, HEAD_DIM), b16),
+            pltpu.VMEM((slab, width), b16),
+            pltpu.VMEM((seq, 2, half, width), b16),
+            pltpu.VMEM((head - 1, rows, features), b16),
+            pltpu.VMEM((head - 1, rows, features), b16),
+            pltpu.VMEM((rows, features), f32),
+            pltpu.VMEM((3 * TT, TILE, slab), f32),
+            pltpu.VMEM((3 * TT, TILE, slab), b16),
+            dma((4, heads, head - 1)),
+            dma((4, heads, head - 1)),
+            dma((4, heads)),
+            dma((2, 2, heads)),
+            dma((2, 2, heads)),
+            dma((2, 2, heads)),
+            dma((2, 2, heads)),
+            dma((seq - 1,)),
+            dma((seq - 1,)),
+            dma((seq - 1,)),
+            dma((seq - 1,)),
+            dma((2,)),
+            dma((head - 1,)),
+            dma((head - 1,)),
+        ],
+        compiler_params=pltpu.CompilerParams(
+            collective_id=0, has_side_effects=True, vmem_limit_bytes=56 * 2**20
+        ),
+        name="whole",
+    )(bias, key_rows, value_rows, query_rows, grad_rows, out_weight)
+
+
 def body(query_rows, key_rows, value_rows, grad_rows, tile_offsets, out_weight):
     seq = lax.axis_size("seq")
     moves, steps = routes_of(seq // TH)
     bias = live_bias(tile_offsets, lax.axis_index("seq"), steps)
+    if seq == 2 * TH and lax.axis_size("groups") == 2:
+        return tuple(whole(bias, key_rows, value_rows, query_rows, grad_rows, out_weight))
     weight = lax.all_gather(out_weight, "seq", axis=0, tiled=True)
     key_h, value_h, query_h, grad_h = (
         lax.all_to_all(rows, "head", split_axis=1, concat_axis=0, tiled=True)

time: 187 us -> 132 us (0.71)
  waiting for transfers between devices: 112 us -> 0 us
  Pallas kernels: 17.3 us -> 124 us
  starting transfers between devices: 25.7 us -> 0 us
  between operations: 14.2 us -> 0.69 us
  matrix products: 4.36 us -> 0 us
  other arithmetic: 3.51 us -> 0.28 us
  local copies, waits for them, and re-layouts: 9.57 us -> 6.6 us
    pallas_call x1, Pallas kernels: 17.3 us -> 124 us  [whole(): pl.pallas_call(functools.partial(whole_kernel, groups, seq, head), in_spe...]
    ppermute x8 -> x0, waiting for transfers between devices: 84.4 us -> none  [the longest x4 42.9 us: settle(): total = total + lax.ppermute(term, 'seq', back).astype(jnp.float32)]
    all_to_all x4 -> x0, waiting for transfers between devices: 26.9 us -> none  [body(): lax.all_to_all(rows, 'head', split_axis=1, concat_axis=0, tiled=True)]
    all_to_all x4 -> x0, starting transfers between devices: 14.8 us -> none  [body(): lax.all_to_all(rows, 'head', split_axis=1, concat_axis=0, tiled=True)]
    ppermute x8 -> x0, starting transfers between devices: 10.8 us -> none  [the longest x4 5.52 us: settle(): total = total + lax.ppermute(term, 'seq', back).astype(jnp.float32)]
    all_to_all x4 -> x0, local copies, waits for them, and re-layouts: 4.46 us -> none  [body(): lax.all_to_all(rows, 'head', split_axis=1, concat_axis=0, tiled=True)]
    dot_general x1 -> x0, matrix products: 4.36 us -> none  [dot(): lax.dot_general(a, b, (((ca,), (cb,)), ((), ())), preferred_element_type=...]
    convert_element_type x2 -> x0, other arithmetic: 3.24 us -> none  [settle(): return total.astype(jnp.bfloat16)]
  transfers between devices with their start and end apart: 14 -> 0, of which waited for: 10 -> 0; matrix products, arithmetic and copies ran while one was open for 4% -> 0% of each run, Pallas kernels for 9% -> 0%
where the time goes in v2:
time: 132 us
  Pallas kernels  124 us (94%)
  local copies, waits for them, and re-layouts  6.6 us (5%)
    pallas_call x1, Pallas kernels, whole(): pl.pallas_call(functools.partial(whole_kernel, groups, seq, head), in_spe...  124 us
    unnamed x14, local copies, waits for them, and re-layouts  6.56 us

profile of v2, /device:TPU:0, one launch (start us, length us, event | category | flops | bytes accessed | tf_op | source)
XLA Modules:
  0.0 131.6 jit_solution(6942263683772342512)
XLA Ops:
  0.6 0.0 copy-start.3
  0.7 0.7 copy-done.3
  1.3 0.1 bitcast_compare_fusion.1
  1.4 0.2 fusion.1
  1.7 0.1 broadcast_bitcast_fusion
  1.7 0.6 copy.10
  2.4 124.1 %whole.1 = (bf16[128,2048]{1,0:T(8,128)(2,1)}, bf16[512,512]{1,0:T(8,128)(2,1)}, bf16[512,512]{1,0:T(8,128)(2,1)}, bf16[512,512]{1,0:T(8,128)(2,1)}) custom-call(f32[6,512]{1,0:T(8,128)} %bitcast.50, bf16[128,2048]{1,0:T(8,128)(2,1)} %refs_1_.1, bf16[128,2048]{1,0:T(8,128)(2,1)} %refs_2_.1, bf16[128,2048]{1,0:T(8,128)(2,1)} %refs_3_.1, ...), custom_call_target="tpu_custom_call" | custom-call | tf_op jit(solution)/shard_map/whole/pallas_call | solution.py:374
  126.4 0.0 copy-start.2
  126.4 1.9 %copy.15 = bf16[128,2048]{1,0:T(8,128)(2,1)} copy(bf16[128,2048]{1,0:T(8,128)(2,1)} %get-tuple-element.20) | data formatting | bytes 1048576
  128.4 0.0 copy-done.2
  128.4 0.0 copy-start.1
  128.4 0.8 copy.16
  129.2 0.4 copy-done.1
  129.6 0.0 copy-start
  129.6 0.8 copy.17
  130.4 0.4 copy-done
  130.9 0.8 copy.18
  (4 shorter events, 0.1 us)
Async XLA Ops:
  0.6 0.7 copy-start.3
  126.4 2.0 %copy-start.2 = (bf16[512,512]{1,0:T(8,128)(2,1)S(1)}, bf16[512,512]{1,0:T(8,128)(2,1)}, u32[]{:S(2)}) copy-start(bf16[512,512]{1,0:T(8,128)(2,1)} %get-tuple-element.21) | copy-start | bytes 1572868
  128.4 1.2 copy-start.1
  129.6 1.2 copy-start

commit v3 on v2

--- a/solution.py
+++ b/solution.py
@@ -146,10 +146,10 @@
 
 
 def whole_kernel(groups, seq, head, *refs):
-    bias_ref, k_in, v_in, q_in, g_in, w_in = refs[:6]
+    offsets, k_in, v_in, q_in, g_in, w_in = refs[:6]
     proj_ref, dq_ref, dk_ref, dv_ref = refs[6:10]
-    mine, near, d_self, d_out, d_in, att, weight, p_out, p_in, p_self, s_scr, w_scr = refs[10:22]
-    (x_send, x_recv, x_own, n_send, n_recv, d_send, d_recv, z_send, z_recv, y_send, y_recv, w_own, p_send, p_recv) = refs[22:]
+    mine, near, d_self, d_out, d_in, att, weight, p_out, p_in, p_self, s_scr, w_scr, bias_ref = refs[10:23]
+    (x_send, x_recv, x_own, n_send, n_recv, d_send, d_recv, z_send, z_recv, y_send, y_recv, w_own, p_send, p_recv) = refs[23:]
     inputs = (k_in, v_in, q_in, g_in)
     heads, slab = mine.shape[1], mine.shape[2]
     rows = k_in.shape[0]
@@ -244,9 +244,9 @@
             head_move(a, h, i, before(i)).wait_recv()
         head_own(a, h).wait()
 
-    send_inputs((0, 1))
     for i in range(1, seq):
         weight_z(i, me_s).start()
+    send_inputs((0, 1))
     send_inputs((2, 3))
     for part in range(2):
         weight_own(part).start()
@@ -259,9 +259,18 @@
         return carry
 
     lax.fori_loop(0, heads, pass_on, 0)
-    for i in range(1, seq):
-        weight_z(i, lax.rem(me_s + seq - i, seq)).wait_recv()
-        weight_y(i, me_g).start()
+
+    step_r, step_c = 1 - 2 * lax.rem(me_s, TH), 1 - 2 * (me_s // TH)
+    for c in range(TT):
+        slots = [[offsets[c, w, x] for x in range(3)] for w in range(offsets.shape[1])]
+        for r, (want_r, want_c) in enumerate(((0, 0), (step_r, 0), (0, step_c))):
+            for t in range(TT):
+                found = None
+                for o_t, o_r, o_c in slots:
+                    hit = (o_t == t - c) & (o_r == want_r) & (o_c == want_c)
+                    found = hit if found is None else found | hit
+                level = jnp.where(found, 0.0, DEAD).astype(jnp.float32)
+                bias_ref[r * TT + t : r * TT + t + 1, c * TILE : (c + 1) * TILE] = jnp.full((1, TILE), level)
 
     def work(h, carry):
         take_inputs(2, h)
@@ -298,6 +307,13 @@
         for a in range(2):
             for j in (1, 0):
                 grad_move(j, a, h).start()
+
+        @pl.when(h == heads // 2 - 1)
+        def _():
+            for i in range(1, seq):
+                weight_z(i, lax.rem(me_s + seq - i, seq)).wait_recv()
+                weight_y(i, me_g).start()
+
         return carry
 
     lax.fori_loop(0, heads, work, 0)
@@ -362,7 +378,7 @@
         term_move(i).wait_send()
 
 
-def whole(bias, key_rows, value_rows, query_rows, grad_rows, out_weight):
+def whole(tile_offsets, key_rows, value_rows, query_rows, grad_rows, out_weight):
     groups, seq, head = (lax.axis_size(name) for name in ("groups", "seq", "head"))
     rows, features = key_rows.shape
     slab, width = rows * head, features // head
@@ -373,7 +389,7 @@
     grads = jax.ShapeDtypeStruct((slab, width), b16)
     return pl.pallas_call(
         functools.partial(whole_kernel, groups, seq, head),
-        in_specs=[vmem] + [pl.BlockSpec(memory_space=pl.ANY)] * 5,
+        in_specs=[pl.BlockSpec(memory_space=pltpu.SMEM)] + [pl.BlockSpec(memory_space=pl.ANY)] * 5,
         out_specs=[vmem] * 4,
         out_shape=[jax.ShapeDtypeStruct((rows, features), b16), grads, grads, grads],
         scratch_shapes=[
@@ -389,6 +405,7 @@
             pltpu.VMEM((rows, features), f32),
             pltpu.VMEM((3 * TT, TILE, slab), f32),
             pltpu.VMEM((3 * TT, TILE, slab), b16),
+            pltpu.VMEM((3 * TT, slab), f32),
             dma((4, heads, head - 1)),
             dma((4, heads, head - 1)),
             dma((4, heads)),
@@ -408,15 +425,15 @@
             collective_id=0, has_side_effects=True, vmem_limit_bytes=56 * 2**20
         ),
         name="whole",
-    )(bias, key_rows, value_rows, query_rows, grad_rows, out_weight)
+    )(tile_offsets, key_rows, value_rows, query_rows, grad_rows, out_weight)
 
 
 def body(query_rows, key_rows, value_rows, grad_rows, tile_offsets, out_weight):
     seq = lax.axis_size("seq")
     moves, steps = routes_of(seq // TH)
+    if seq == 2 * TH and lax.axis_size("groups") == 2:
+        return tuple(whole(tile_offsets, key_rows, value_rows, query_rows, grad_rows, out_weight))
     bias = live_bias(tile_offsets, lax.axis_index("seq"), steps)
-    if seq == 2 * TH and lax.axis_size("groups") == 2:
-        return tuple(whole(bias, key_rows, value_rows, query_rows, grad_rows, out_weight))
     weight = lax.all_gather(out_weight, "seq", axis=0, tiled=True)
     key_h, value_h, query_h, grad_h = (
         lax.all_to_all(rows, "head", split_axis=1, concat_axis=0, tiled=True)

time: 132 us -> 132 us (level)
    unnamed x14 -> x11, local copies, waits for them, and re-layouts: 6.56 us -> 6.56 us
where the time goes in v3:
time: 132 us; the launch traced here: 131 us
  Pallas kernels  124 us (94%)
  local copies, waits for them, and re-layouts  6.56 us (5%)
    pallas_call x1, Pallas kernels, whole(): pl.pallas_call(functools.partial(whole_kernel, groups, seq, head), in_spe...  124 us
    unnamed x11, local copies, waits for them, and re-layouts  6.56 us

profile of v3, /device:TPU:0, one launch (start us, length us, event | category | flops | bytes accessed | tf_op | source)
XLA Modules:
  0.0 131.3 jit_solution(674143824516614233)
XLA Ops:
  0.6 1.4 %copy.10.refs_0_ = s32[2,7,3]{2,1,0:T(8,128)} copy(s32[2,7,3]{1,0,2:T(2,128)} %param.10) | data formatting | bytes 336 | tf_op args[4]
  2.0 124.1 %whole.1 = (bf16[128,2048]{1,0:T(8,128)(2,1)}, bf16[512,512]{1,0:T(8,128)(2,1)}, bf16[512,512]{1,0:T(8,128)(2,1)}, bf16[512,512]{1,0:T(8,128)(2,1)}) custom-call(s32[2,7,3]{2,1,0:T(8,128)} %copy.10.refs_0_, bf16[128,2048]{1,0:T(8,128)(2,1)} %refs_1_.1, bf16[128,2048]{1,0:T(8,128)(2,1)} %refs_2_.1, bf16[128,2048]{1,0:T(8,128)(2,1)} %refs_3_.1, ...), custom_call_target="tpu_custom_call" | custom-call | tf_op jit(solution)/shard_map/whole/pallas_call | solution.py:390
  126.1 0.0 copy-start.2
  126.1 1.9 %copy.15 = bf16[128,2048]{1,0:T(8,128)(2,1)} copy(bf16[128,2048]{1,0:T(8,128)(2,1)} %get-tuple-element.8) | data formatting | bytes 1048576
  128.0 0.0 copy-done.2
  128.0 0.0 copy-start.1
  128.0 0.8 copy.16
  128.8 0.4 copy-done.1
  129.3 0.0 copy-start
  129.3 0.8 copy.17
  130.1 0.4 copy-done
  130.5 0.8 copy.18
Async XLA Ops:
  126.1 2.0 %copy-start.2 = (bf16[512,512]{1,0:T(8,128)(2,1)S(1)}, bf16[512,512]{1,0:T(8,128)(2,1)}, u32[]{:S(2)}) copy-start(bf16[512,512]{1,0:T(8,128)(2,1)} %get-tuple-element.9) | copy-start | bytes 1572868
  128.0 1.2 copy-start.1
  129.3 1.2 copy-start

commit v4 on v3

--- a/solution.py
+++ b/solution.py
@@ -192,11 +192,11 @@
             inputs[a].at[:, columns(me_h, h)], mine.at[a, h, row_block(me_h), :], x_own.at[a, h]
         )
 
-    def near_move(j, a, h):
-        return remote(mine.at[a, h], near.at[j, a, h], n_send.at[j, a, h], n_recv.at[j, a, h], at(s=beside[j]))
-
-    def grad_move(j, a, h):
-        return remote(d_out.at[j, a, h], d_in.at[j, a, h], d_send.at[j, a, h], d_recv.at[j, a, h], at(s=beside[j]))
+    def near_move(j, h):
+        return remote(mine.at[0:2, h], near.at[j, :, h], n_send.at[j, h], n_recv.at[j, h], at(s=beside[j]))
+
+    def grad_move(j, h):
+        return remote(d_out.at[j, :, h], d_in.at[j, :, h], d_send.at[j, h], d_recv.at[j, h], at(s=beside[j]))
 
     def weight_z(i, owner):
         return remote(
@@ -254,8 +254,8 @@
     def pass_on(h, carry):
         for a in range(2):
             take_inputs(a, h)
-            for j in (1, 0):
-                near_move(j, a, h).start()
+        for j in (1, 0):
+            near_move(j, h).start()
         return carry
 
     lax.fori_loop(0, heads, pass_on, 0)
@@ -276,8 +276,7 @@
         take_inputs(2, h)
         take_inputs(3, h)
         for j in range(2):
-            for a in range(2):
-                near_move(j, a, h).wait_recv()
+            near_move(j, h).wait_recv()
 
         def tile(b):
             return slice((b % TT) * TILE, (b % TT + 1) * TILE)
@@ -304,9 +303,8 @@
         )
         att[:, columns(0, h)] = attended
         dq_ref[:, columns(0, h)] = dq
-        for a in range(2):
-            for j in (1, 0):
-                grad_move(j, a, h).start()
+        for j in (1, 0):
+            grad_move(j, h).start()
 
         @pl.when(h == heads // 2 - 1)
         def _():
@@ -344,10 +342,11 @@
     project(me_h, to_keep)
 
     def settle(h, carry):
+        for j in range(2):
+            grad_move(j, h).wait_recv()
         for a, out in ((1, dv_ref), (0, dk_ref)):
             total = d_self[a, h]
             for j in range(2):
-                grad_move(j, a, h).wait_recv()
                 total = total + d_in[j, a, h].astype(jnp.float32)
             out[:, columns(0, h)] = total.astype(jnp.bfloat16)
         return carry
@@ -364,10 +363,9 @@
         for a in range(4):
             for i in range(1, head):
                 head_move(a, h, i, me_h).wait_send()
-        for a in range(2):
-            for j in range(2):
-                near_move(j, a, h).wait_send()
-                grad_move(j, a, h).wait_send()
+        for j in range(2):
+            near_move(j, h).wait_send()
+            grad_move(j, h).wait_send()
         return carry
 
     lax.fori_loop(0, heads, drain, 0)
@@ -409,10 +407,10 @@
             dma((4, heads, head - 1)),
             dma((4, heads, head - 1)),
             dma((4, heads)),
-            dma((2, 2, heads)),
-            dma((2, 2, heads)),
-            dma((2, 2, heads)),
-            dma((2, 2, heads)),
+            dma((2, heads)),
+            dma((2, heads)),
+            dma((2, heads)),
+            dma((2, heads)),
             dma((seq - 1,)),
             dma((seq - 1,)),
             dma((seq - 1,)),

time: 132 us -> 131 us (level)
  no operation moved by 1% of the time
where the time goes in v4:
time: 131 us
  Pallas kernels  123 us (94%)
  local copies, waits for them, and re-layouts  6.56 us (5%)
    pallas_call x1, Pallas kernels, whole(): pl.pallas_call(functools.partial(whole_kernel, groups, seq, head), in_spe...  123 us
    unnamed x11, local copies, waits for them, and re-layouts  6.56 us

profile of v4, /device:TPU:0, one launch (start us, length us, event | category | flops | bytes accessed | tf_op | source)
XLA Modules:
  0.0 130.7 jit_solution(7089912294188353060)
XLA Ops:
  0.6 1.4 %copy.10.refs_0_ = s32[2,7,3]{2,1,0:T(8,128)} copy(s32[2,7,3]{1,0,2:T(2,128)} %param.10) | data formatting | bytes 336 | tf_op args[4]
  2.0 123.5 %whole.1 = (bf16[128,2048]{1,0:T(8,128)(2,1)}, bf16[512,512]{1,0:T(8,128)(2,1)}, bf16[512,512]{1,0:T(8,128)(2,1)}, bf16[512,512]{1,0:T(8,128)(2,1)}) custom-call(s32[2,7,3]{2,1,0:T(8,128)} %copy.10.refs_0_, bf16[128,2048]{1,0:T(8,128)(2,1)} %refs_1_.1, bf16[128,2048]{1,0:T(8,128)(2,1)} %refs_2_.1, bf16[128,2048]{1,0:T(8,128)(2,1)} %refs_3_.1, ...), custom_call_target="tpu_custom_call" | custom-call | tf_op jit(solution)/shard_map/whole/pallas_call | solution.py:388
  125.5 0.0 copy-start.2
  125.5 1.9 %copy.15 = bf16[128,2048]{1,0:T(8,128)(2,1)} copy(bf16[128,2048]{1,0:T(8,128)(2,1)} %get-tuple-element.8) | data formatting | bytes 1048576
  127.4 0.0 copy-done.2
  127.4 0.0 copy-start.1
  127.5 0.8 copy.16
  128.2 0.4 copy-done.1
  128.7 0.0 copy-start
  128.7 0.8 copy.17
  129.5 0.4 copy-done
  129.9 0.8 copy.18
Async XLA Ops:
  125.5 2.0 %copy-start.2 = (bf16[512,512]{1,0:T(8,128)(2,1)S(1)}, bf16[512,512]{1,0:T(8,128)(2,1)}, u32[]{:S(2)}) copy-start(bf16[512,512]{1,0:T(8,128)(2,1)} %get-tuple-element.9) | copy-start | bytes 1572868
  127.4 1.2 copy-start.1
  128.7 1.2 copy-start

commit v5 on v4

--- a/solution.py
+++ b/solution.py
@@ -254,7 +254,7 @@
     def pass_on(h, carry):
         for a in range(2):
             take_inputs(a, h)
-        for j in (1, 0):
+        for j in range(2):
             near_move(j, h).start()
         return carry
 
@@ -303,7 +303,7 @@
         )
         att[:, columns(0, h)] = attended
         dq_ref[:, columns(0, h)] = dq
-        for j in (1, 0):
+        for j in range(2):
             grad_move(j, h).start()
 
         @pl.when(h == heads // 2 - 1)

time: 131 us -> 131 us (level)
  no operation moved by 1% of the time
where the time goes in v5:
time: 131 us
  Pallas kernels  124 us (95%)
  local copies, waits for them, and re-layouts  6.56 us (5%)
    pallas_call x1, Pallas kernels, whole(): pl.pallas_call(functools.partial(whole_kernel, groups, seq, head), in_spe...  124 us
    unnamed x11, local copies, waits for them, and re-layouts  6.56 us

profile of v5, /device:TPU:0, one launch (start us, length us, event | category | flops | bytes accessed | tf_op | source)
XLA Modules:
  0.0 130.7 jit_solution(17758313675050327706)
XLA Ops:
  0.6 1.4 %copy.10.refs_0_ = s32[2,7,3]{2,1,0:T(8,128)} copy(s32[2,7,3]{1,0,2:T(2,128)} %param.10) | data formatting | bytes 336 | tf_op args[4]
  2.0 123.5 %whole.1 = (bf16[128,2048]{1,0:T(8,128)(2,1)}, bf16[512,512]{1,0:T(8,128)(2,1)}, bf16[512,512]{1,0:T(8,128)(2,1)}, bf16[512,512]{1,0:T(8,128)(2,1)}) custom-call(s32[2,7,3]{2,1,0:T(8,128)} %copy.10.refs_0_, bf16[128,2048]{1,0:T(8,128)(2,1)} %refs_1_.1, bf16[128,2048]{1,0:T(8,128)(2,1)} %refs_2_.1, bf16[128,2048]{1,0:T(8,128)(2,1)} %refs_3_.1, ...), custom_call_target="tpu_custom_call" | custom-call | tf_op jit(solution)/shard_map/whole/pallas_call | solution.py:388
  125.5 0.0 copy-start.2
  125.6 1.9 %copy.15 = bf16[128,2048]{1,0:T(8,128)(2,1)} copy(bf16[128,2048]{1,0:T(8,128)(2,1)} %get-tuple-element.8) | data formatting | bytes 1048576
  127.5 0.0 copy-done.2
  127.5 0.0 copy-start.1
  127.5 0.8 copy.16
  128.3 0.4 copy-done.1
  128.7 0.0 copy-start
  128.7 0.8 copy.17
  129.5 0.4 copy-done
  130.0 0.8 copy.18
Async XLA Ops:
  125.5 2.0 %copy-start.2 = (bf16[512,512]{1,0:T(8,128)(2,1)S(1)}, bf16[512,512]{1,0:T(8,128)(2,1)}, u32[]{:S(2)}) copy-start(bf16[512,512]{1,0:T(8,128)(2,1)} %get-tuple-element.9) | copy-start | bytes 1572868
  127.5 1.2 copy-start.1
  128.7 1.2 copy-start
